TPU v7x, 512 devices: a whole 4x4x16 slice. The times are simulated.
512 devices in a mesh: dp: 32 (over y, z_hi, core), ctx: 16 (over z_lo, x).
Axes of the slice: x: 4, y: 4, z: 16 (z_hi: 4, z_lo: 4; z = z_hi * 4 + z_lo), core: 2. Of those that a mesh axis runs over, the one named last changes fastest.
Arguments:
- q_lin: bfloat16 [32, 2048, 1792], P('dp', 'ctx'), may hold values from -100 to 100
- k_lin: bfloat16 [32, 2048, 256], P('dp', 'ctx'), may hold values from -12 to 12
- v_lin: bfloat16 [32, 2048, 256], P('dp', 'ctx'), may hold values from -6 to 6
- out_grad: bfloat16 [32, 2048, 1792], P('dp', 'ctx'), may hold values from -6 to 6
- q_bias: float32 [1792], replicated, may hold values from -3 to 3
- doc_lengths: int32 [32, 16], P('dp'), may hold values from 1 to 1152, 2048 in all within a row
Outputs:
- attended: bfloat16 [32, 2048, 1792], P('dp', 'ctx')
- grad_q: bfloat16 [32, 2048, 1792], P('dp', 'ctx')
- grad_k: bfloat16 [32, 2048, 256], P('dp', 'ctx')
- grad_v: bfloat16 [32, 2048, 256], P('dp', 'ctx')
- bias_grad: float32 [1792], replicated
Inputs may be any that keep to these rules, and one draw needn't show every extreme that they name: `doc_lengths`: each row holds 16 document lengths that sum to 2048; the longest is exactly 1152.
All inputs are finite; a program needn't handle non-finite values.
Results may differ from a plain program's by a relative error of at most 0.025.
The roundings to bfloat16 on the way count: a program that leaves them out, or rounds other values in their place, can miss the bound.
Values may be sent and summed in bfloat16 or wider, within the bound.
A program may use at most 64 MiB of HBM per device.

v0:
```python
import math

import jax
import jax.numpy as jnp
from jax import lax
from jax.sharding import PartitionSpec as P

HD = 128


rope_theta = 1000000.0
neg_fill = -1e30


def rope_tables(positions, head_size):
    half_size = head_size // 2
    exponent = jnp.arange(half_size, dtype=jnp.float32) * (2.0 / head_size)
    inverse_freq = jnp.power(jnp.float32(rope_theta), -exponent)
    angles = positions.astype(jnp.float32)[:, None] * inverse_freq[None, :]
    cosine = jnp.concatenate([jnp.cos(angles), jnp.cos(angles)], axis=1)
    sine_table = jnp.concatenate([jnp.sin(angles), jnp.sin(angles)], axis=1)
    return (cosine, sine_table)


def rotate(vectors, cosine, sine_table, direction):
    half_size = vectors.shape[-1] // 2
    turned = jnp.concatenate([-vectors[..., half_size:], vectors[..., :half_size]], axis=-1)
    return vectors * cosine[:, None, :] + direction * turned * sine_table[:, None, :]


def doc_starts(lengths, positions):
    doc_ends = jnp.cumsum(lengths)
    before = jnp.where(doc_ends[None, :] <= positions[:, None], lengths[None, :], 0)
    return jnp.sum(before, axis=1)


def keep_same(current, key_block, value_block, offset):
    return current


def shards(q_lin, k_lin, v_lin, out_grad, q_bias, doc_lengths):
    row_count = q_lin.shape[1]
    q_heads = q_lin.shape[2] // HD
    kv_heads = k_lin.shape[2] // HD
    group_size = q_heads // kv_heads
    score_scale = 1.0 / math.sqrt(HD)
    ctx_size = lax.axis_size("ctx")
    seq_len = row_count * ctx_size
    block_rows = row_count * math.gcd(ctx_size, max(1, 512 // row_count))
    block_total = seq_len // block_rows
    first_row = lax.axis_index("ctx") * row_count
    row_pos = first_row + jnp.arange(row_count, dtype=jnp.int32)
    row_start = doc_starts(doc_lengths[0], row_pos)
    cosine, sine_table = rope_tables(row_pos - row_start, HD)
    shifted = (q_lin[0].astype(jnp.float32) + q_bias).reshape(row_count, q_heads, HD)
    query_heads = (
        rotate(shifted, cosine, sine_table, 1.0)
        .astype(jnp.bfloat16)
        .reshape(row_count, kv_heads, group_size, HD)
    )
    rotated_keys = (
        rotate(
            k_lin[0].astype(jnp.float32).reshape(row_count, kv_heads, HD), cosine, sine_table, 1.0
        )
        .astype(jnp.bfloat16)
        .reshape(row_count, kv_heads * HD)
    )
    values = v_lin[0]
    grad_rows = out_grad[0].reshape(row_count, kv_heads, group_size, HD)
    last_row = first_row + row_count - 1
    earliest = row_start[0]

    def scored(key_block, offset):
        block_size = key_block.shape[0]
        key_heads = key_block.reshape(block_size, kv_heads, HD)
        scores = (
            jnp.einsum("rkgd,nkd->kgrn", query_heads, key_heads, preferred_element_type=jnp.float32)
            * score_scale
        )
        key_pos = offset + jnp.arange(block_size, dtype=jnp.int32)
        visible_mask = (key_pos[None, :] <= row_pos[:, None]) & (
            key_pos[None, :] >= row_start[:, None]
        )
        return (key_heads, scores, visible_mask)

    def guarded(step_fn, skip_fn, current, key_block, value_block, offset):
        is_visible = (offset <= last_row) & (offset + key_block.shape[0] - 1 >= earliest)
        return lax.cond(
            is_visible,
            lambda current_state: step_fn(current_state, key_block, value_block, offset),
            lambda current_state: skip_fn(current_state, key_block, value_block, offset),
            current,
        )

    def stats_step(running, key_block, value_block, offset):
        key_heads, scores, visible_mask = scored(key_block, offset)
        run_max, run_sum = running
        block_max = jnp.max(jnp.where(visible_mask, scores, neg_fill), axis=-1)
        new_max = jnp.maximum(run_max, block_max)
        exp_terms = jnp.where(visible_mask, jnp.exp(scores - new_max[..., None]), 0.0)
        return (new_max, jnp.sum(exp_terms, axis=-1))

    stats_init = (
        jnp.full((kv_heads, group_size, row_count), neg_fill, jnp.float32),
        jnp.zeros((kv_heads, group_size, row_count), jnp.float32),
    )
    all_keys = rotated_keys
    all_values = values
    run_max, run_sum = guarded(
        stats_step,
        keep_same,
        stats_init,
        lax.all_gather(rotated_keys, "ctx", axis=0, tiled=True),
        None,
        jnp.int32(0),
    )
    log_total = run_max + jnp.log(run_sum)

    def weighted(scores, visible_mask):
        return jnp.where(visible_mask, jnp.exp(scores - log_total[..., None]), 0.0).astype(
            jnp.bfloat16
        )

    def out_step(accum, key_block, value_block, offset):
        key_heads, scores, visible_mask = scored(key_block, offset)
        weights = weighted(scores, visible_mask)
        value_heads = value_block.reshape(value_block.shape[0], kv_heads, HD)
        return jnp.einsum(
            "kgrn,nkd->rkgd", weights, value_heads, preferred_element_type=jnp.float32
        )

    out_init = jnp.zeros((row_count, kv_heads, group_size, HD), jnp.float32)
    accum = guarded(
        out_step,
        keep_same,
        out_init,
        lax.all_gather(rotated_keys, "ctx", axis=0, tiled=True),
        lax.all_gather(values, "ctx", axis=0, tiled=True),
        jnp.int32(0),
    )
    all_keys, all_values = (
        lax.all_gather(rotated_keys, "ctx", axis=0, tiled=True),
        lax.all_gather(values, "ctx", axis=0, tiled=True),
    )
    attended = accum.astype(jnp.bfloat16)
    row_delta = jnp.sum(
        grad_rows.astype(jnp.float32) * attended.astype(jnp.float32), axis=-1
    ).transpose(1, 2, 0)

    def grad_step(grad_acc, key_block, value_block, offset):
        key_heads, scores, visible_mask = scored(key_block, offset)
        weights = weighted(scores, visible_mask)
        block_size = key_block.shape[0]
        value_heads = value_block.reshape(block_size, kv_heads, HD)
        grad_prob = jnp.einsum(
            "rkgd,nkd->kgrn", grad_rows, value_heads, preferred_element_type=jnp.float32
        )
        dscore = (weights.astype(jnp.float32) * (grad_prob - row_delta[..., None])).astype(
            jnp.bfloat16
        )
        new_acc = grad_acc + jnp.einsum(
            "kgrn,nkd->rkgd", dscore, key_heads, preferred_element_type=jnp.float32
        )
        key_term = score_scale * jnp.einsum(
            "kgrn,rkgd->nkd", dscore, query_heads, preferred_element_type=jnp.float32
        )
        value_term = jnp.einsum(
            "kgrn,rkgd->nkd", weights, grad_rows, preferred_element_type=jnp.float32
        )
        return (
            new_acc,
            key_term.reshape(block_size, kv_heads * HD),
            value_term.reshape(block_size, kv_heads * HD),
        )

    def skip_grad(grad_acc, key_block, value_block, offset):
        zero_term = jnp.zeros((key_block.shape[0], kv_heads * HD), jnp.float32)
        return (grad_acc, zero_term, zero_term)

    grad_init = jnp.zeros((row_count, kv_heads, group_size, HD), jnp.float32)

    def grad_loop(grad_acc, block_index):
        offset = block_index * block_rows
        key_block = lax.dynamic_slice_in_dim(all_keys, offset, block_rows, 0)
        value_block = lax.dynamic_slice_in_dim(all_values, offset, block_rows, 0)
        new_acc, key_term, value_term = guarded(
            grad_step, skip_grad, grad_acc, key_block, value_block, offset
        )
        return (new_acc, (key_term, value_term))

    grad_acc, stacked = lax.scan(grad_loop, grad_init, jnp.arange(block_total, dtype=jnp.int32))
    key_terms = stacked[0].reshape(seq_len, kv_heads * HD)
    value_terms = stacked[1].reshape(seq_len, kv_heads * HD)
    summed = (
        lax.psum_scatter(
            key_terms.astype(jnp.bfloat16), "ctx", scatter_dimension=0, tiled=True
        ).astype(jnp.float32),
        lax.psum_scatter(
            value_terms.astype(jnp.bfloat16), "ctx", scatter_dimension=0, tiled=True
        ).astype(jnp.float32),
    )
    grad_pre = rotate(
        (score_scale * grad_acc).reshape(row_count, q_heads, HD), cosine, sine_table, -1.0
    )
    bias_part = jnp.sum(grad_pre, axis=0).reshape(-1)
    bias_total = lax.psum(bias_part, ("dp", "ctx"))
    token_total = seq_len * lax.axis_size("dp")
    bias_grad = bias_total / math.sqrt(token_total)
    grad_key = rotate(summed[0].reshape(row_count, kv_heads, HD), cosine, sine_table, -1.0).astype(
        jnp.bfloat16
    )
    grad_value = summed[1].astype(jnp.bfloat16)
    attended_out = attended.reshape(1, row_count, q_heads * HD)
    grad_q = grad_pre.astype(jnp.bfloat16).reshape(1, row_count, q_heads * HD)
    grad_k = grad_key.reshape(1, row_count, kv_heads * HD)
    grad_v = grad_value.reshape(1, row_count, kv_heads * HD)
    return (attended_out, grad_q, grad_k, grad_v, bias_grad)


def solution(mesh):
    placed = (
        P("dp", "ctx", None),
        P("dp", "ctx", None),
        P("dp", "ctx", None),
        P("dp", "ctx", None),
        P(),
        P("dp", None),
    )
    return jax.shard_map(
        shards,
        mesh=mesh,
        in_specs=placed,
        out_specs=(
            P("dp", "ctx", None),
            P("dp", "ctx", None),
            P("dp", "ctx", None),
            P("dp", "ctx", None),
            P(),
        ),
        check_vma=False,
    )
```

profile of v0, /device:TPU:16, one launch (start us, length us, event | category | flops | bytes accessed | tf_op | source)
XLA Modules:
  0.0 410.4 jit_solution(15872081450161948341)
XLA Ops:
  7.2 0.8 copy.73
  8.2 0.7 select_reduce_fusion
  9.1 0.7 broadcast_multiply_fusion.1
  9.9 0.9 reshape.230
  11.4 1.5 fusion.38
  13.0 1.6 copy.78
  14.6 1.3 copy.76
  17.0 86.5 %all-gather.4.cloned.1.call-done = bf16[2048,256]{1,0:T(8,128)(2,1)} async-done(((bf16[128,256]{1,0:T(8,128)(2,1)}), bf16[2048,256]{1,0:T(8,128)(2,1)}) %all-gather.4.cloned.1.call-update) | async-done | bytes 1048592 | tf_op jit(solution)/shard_map/all_gather | solution.py:137
  103.5 16.8 %conditional.3 = (f32[2,7,128]{2,1,0:T(8,128)}, f32[2,7,128]{2,1,0:T(8,128)S(1)}) conditional(s32[]{:T(128)} %convert_element_type.127, () %tuple.81, (s32[128]{0:T(128)S(1)}, s32[128]{0:T(128)S(1)}, bf16[2048,256]{1,0:T(8,128)(2,1)}, bf16[128,2,7,128]{0,3,2,1:T(8,128)(2,1)S(1)}) %tuple.82), branch_computations={%region_2.3_spmd, %region_3.6_spmd} | conditional | flops 965998848 | bytes 33802256 | solution.py:88
  103.8 1.3 reshape.208
  105.1 6.5 %fusion.2 = (f32[2,7,128]{2,1,0:T(8,128)S(1)}, f32[2,2048,128,7]{2,1,3,0:T(8,128)}) fusion(pred[128,2048]{0,1:T(8,128)(4,1)S(1)} %fusion.8, bf16[128,2,7,128]{0,3,2,1:T(8,128)(2,1)S(1)} %get-tuple-element.569, bf16[2048,2,128,1]{2,1,0,3:T(2,128)(2,1)S(1)} %bitcast.160), kind=kOutput, calls=%fused_computation.3 | convolution fusion | flops 950532352 | bytes 16456704 | tf_op jit(solution)/shard_map/cond/branch_1_fun/rkgd,nkd->kgrn/dot_general | solution.py:77
  111.6 0.6 broadcast_maximum_fusion
  112.2 8.1 %fusion.5 = f32[2,7,128]{2,1,0:T(8,128)S(1)} fusion(f32[2,2048,128,7]{2,1,3,0:T(8,128)} %get-tuple-element.631, f32[2,7,128]{2,1,0:T(8,128)} %broadcast_maximum_fusion, pred[128,2048]{0,1:T(8,128)(4,1)S(1)} %fusion.8), kind=kLoop, calls=%fused_computation.6 | loop fusion | flops 14678272 | bytes 14956544 | tf_op jit(solution)/shard_map/cond/branch_1_fun/reduce_sum | solution.py:101
  120.3 1.3 add.132
  121.6 55.8 %all-gather.6.cloned.1.call-done = bf16[1,2048,256]{1,2,0:T(8,128)(2,1)} async-done(((bf16[1,128,256]{1,2,0:T(8,128)(2,1)}), bf16[1,2048,256]{1,2,0:T(8,128)(2,1)}) %all-gather.6.cloned.1.call-update) | async-done | bytes 1048592 | tf_op jit(solution)/shard_map/all_gather | solution.py:138
  177.4 7.9 %conditional.4 = (f32[128,2,7,128]{0,3,2,1:T(8,128)S(1)}, bf16[1,128,1792]{2,1,0:T(8,128)(2,1)S(1)}) conditional(s32[]{:T(128)} %convert_element_type.127, () %tuple.80, (s32[128]{0:T(128)S(1)}, s32[128]{0:T(128)S(1)}, bf16[2048,256]{1,0:T(8,128)(2,1)}, bf16[128,2,7,128]{0,3,2,1:T(8,128)(2,1)S(1)}, f32[2,7,128]{2,1,0:T(8,128)}, ...), branch_computations={%region_6.7_spmd, %region_7.8_spmd} | conditional | flops 1894973440 | bytes 7479312 | solution.py:88
  177.4 1.3 reshape.210
  178.8 0.9 fusion.22
  179.7 5.2 %bitcast_convert_fusion = (f32[128,2,7,128]{0,3,2,1:T(8,128)S(1)}, bf16[2,7,128,128]{2,3,1,0:T(8,128)(2,1)S(1)}) fusion(bf16[2048,2,128,1]{0,2,3,1:T(8,128)(2,1)} %bitcast.167, f32[2,7,128]{2,1,0:T(8,128)} %get-tuple-element.435, pred[128,2048]{0,1:T(8,128)(4,1)} %fusion.22, bf16[128,2,7,128]{0,3,2,1:T(8,128)(2,1)S(1)} %get-tuple-element.573, ...), kind=kOutput, calls=%fused_computation.25 | convolution fusion | flops 1894187008 | bytes 4201472 | tf_op jit(solution)/shard_map/cond/branch_1_fun/kgrn,nkd->rkgd/dot_general | solution.py:128
  185.4 0.8 copy-done.5
  186.2 1.5 copy.81
  187.8 18.1 %while.22 = (s32[]{:T(128)}, f32[128,2,7,128]{3,0,2,1:T(8,128)S(1)}, bf16[4,512,256]{1,2,0:T(8,128)(2,1)}, bf16[4,512,256]{1,2,0:T(8,128)(2,1)}, s32[4]{0:T(128)...) while((s32[]{:T(128)}, ...), condition=%wide.region_12.13_spmd.clone, body=%wide.region_9.12_spmd.clone.sunk | while | flops 1182433920 | bytes 18240896 | solution.py:191
  187.8 0.6 dynamic_slice.34
  189.7 7.2 %conditional.7 = (f32[128,2,7,128]{3,0,2,1:T(8,128)S(1)}, bf16[1,512,256]{1,2,0:T(8,128)(2,1)S(1)}, bf16[1,512,256]{1,2,0:T(8,128)(2,1)S(1)}) conditional(s32[]{:T(128)} %convert_element_type.175, f32[128,2,7,128]{3,0,2,1:T(8,128)S(1)} %get-tuple-element.788, (s32[]{:T(128)}, s32[]{:T(128)}, s32[128]{0:T(128)S(1)}, ...), branch_computations={%region_10.10_spmd, %region_11.11_spmd} | conditional | flops 1182433920 | bytes 17190982 | solution.py:88
  189.7 1.2 constant_dynamic-slice_fusion
  190.9 0.6 broadcast_add_fusion
  191.7 1.8 fusion.29
  193.5 0.7 fusion.26
  194.2 1.1 fusion.30
  195.4 0.7 fusion.31
  196.1 0.7 fusion.42
  196.8 0.9 constant_dynamic-update-slice_fusion.3
  199.6 0.8 constant_dynamic-update-slice_fusion.3
  202.3 0.8 constant_dynamic-update-slice_fusion.3
  205.0 0.8 constant_dynamic-update-slice_fusion.3
  205.9 2.4 copy.83
  208.3 1.3 copy.85
  209.9 1.2 copy.82
  211.2 1.3 broadcast_multiply_fusion
  212.5 1.2 copy.87
  213.7 1.2 copy.88
  215.0 1.8 fusion.35
  217.0 1.0 copy.91
  218.0 120.2 %psum.7 = f32[1792]{0:T(1024)S(1)} all-reduce(f32[1792]{0:T(1024)S(1)} %reshape.228), channel_id=1, replica_groups=mesh['dp'=32,'ctx'=16] {'dp','ctx'}, use_global_device_ids=true, to_apply=%region_16.17 | all-reduce | flops 1792 | bytes 14336 | tf_op jit(solution)/shard_map/psum | solution.py:206
  338.2 0.6 broadcast_multiply_fusion.3
  338.8 0.9 reshape.226
  340.1 1.5 fusion.39
  341.6 62.2 %reduce-scatter.5.cloned.1.call-done = bf16[128,256]{1,0:T(8,128)(2,1)} async-done(((bf16[2048,256]{1,0:T(8,128)(2,1)}), bf16[128,256]{1,0:T(8,128)(2,1)}) %reduce-scatter.5.cloned.1.call-update) | async-done | bytes 65552 | tf_op jit(solution)/shard_map/reduce_scatter | solution.py:198
  (75 shorter events, 8.2 us)
Async XLA Ops:
  7.2 8.8 %copy-start.7 = (f32[1792]{0:T(1024)S(1)}, f32[1792]{0:T(1024)}, u32[]{:S(2)}) copy-start(f32[1792]{0:T(1024)} %param.18) | copy-start | bytes 21508
  7.2 8.9 %copy-start.4 = (bf16[1,128,1792]{2,1,0:T(8,128)(2,1)S(1)}, bf16[1,128,1792]{2,1,0:T(8,128)(2,1)}, u32[]{:S(2)}) copy-start(bf16[1,128,1792]{2,1,0:T(8,128)(2,1)} %param.17) | copy-start | bytes 1376260
  7.2 96.3 %all-gather.4.cloned.1.call-start = ((), (), s32[]{:S(2)}) async-start(), calls=%async_computation.2 | async-start | bytes 1114112 | tf_op jit(solution)/shard_map/all_gather | solution.py:137
  9.8 6.9 %copy-start = (f32[128,128]{0,1:T(8,128)}, f32[128,128]{0,1:T(8,128)S(1)}, u32[]{:S(2)}) copy-start(f32[128,128]{0,1:T(8,128)S(1)} %get-tuple-element.647) | copy-start | bytes 196612
  12.9 164.5 %all-gather.6.cloned.1.call-start = ((), (), s32[]{:S(2)}) async-start(), calls=%async_computation.5 | async-start | bytes 1114112 | tf_op jit(solution)/shard_map/all_gather | solution.py:138
  14.6 324.2 %reduce-scatter.3.cloned.1.call-start = ((), (), s32[]{:S(2)}) async-start(), calls=%async_computation.3 | async-start | bytes 1114112 | tf_op jit(solution)/shard_map/reduce_scatter | solution.py:195
  185.4 0.8 copy-start.5
  205.9 2.4 copy-start.2
  205.9 3.8 copy-start.3
  205.9 3.9 copy-start.6
  208.3 195.6 %reduce-scatter.5.cloned.1.call-start = ((), (), s32[]{:S(2)}) async-start(), calls=%async_computation.4 | async-start | bytes 1114112 | tf_op jit(solution)/shard_map/reduce_scatter | solution.py:198
  212.5 4.3 %copy-start.1 = (f32[128,128]{0,1:T(8,128)S(1)}, f32[128,128]{0,1:T(8,128)}, u32[]{:S(2)}) copy-start(f32[128,128]{0,1:T(8,128)} %copy-done) | copy-start | bytes 196612
Sparse Core Ops, SparseCore 0:
  13.0 90.4 all-gather.3
  106.1 71.2 all-gather.5
  208.4 105.1 reduce-scatter.2
  317.0 86.7 reduce-scatter.4
where the time goes:
time: 411 us; the launch traced here: 410 us
  waiting for transfers between devices  205 us (50%)
  blocking collectives  120 us (29%)
  local copies, waits for them, and re-layouts  28.9 us (7%)
  other arithmetic  22.3 us (5%)
  matrix products  16.8 us (4%)
  between operations  14.1 us (3%)
    psum x1, blocking collectives, shards(): bias_total = lax.psum(bias_part, ('dp', 'ctx'))  120 us
    all_gather x1, waiting for transfers between devices, shards(): lax.all_gather(rotated_keys, 'ctx', axis=0, tiled=True)  86.5 us
    reduce_scatter x1, waiting for transfers between devices, shards(): lax.psum_scatter(value_terms.astype(jnp.bfloat16), 'ctx', scatter_dimensi...  62.2 us
    all_gather x1, waiting for transfers between devices, shards(): lax.all_gather(values, 'ctx', axis=0, tiled=True)  55.8 us
    dot_general x2, matrix products, scored(): jnp.einsum('rkgd,nkd->kgrn', query_heads, key_heads, preferred_element_ty...  8.25 us
  transfers between devices with their start and end apart: 4, of which 3 were waited for; matrix products, arithmetic and copies ran while one was open for 8% of the time, Pallas kernels for 0%

commit v1 on v0

v1 whole, which is shorter than its diff:
```python
import math

import jax
import jax.numpy as jnp
import numpy as np
from jax import lax
from jax.experimental import pallas as pl
from jax.experimental.pallas import tpu as pltpu
from jax.sharding import PartitionSpec as P

HD = 128
ROWS = 128
SIDE = 4
WINDOW = 10
SLOTS = 13
PAIRS = WINDOW // 2
THETA = 1000000.0
FILL = -1e30
MESH = pl.DeviceIdType.MESH
F32 = jnp.float32
BF16 = jnp.bfloat16


def dp_stages(size):
    if size == 32:
        return [(1, 2), (2, 4), (8, 4)]
    return [(1, size)] if size > 1 else []


def need(dr, reader, col):
    if dr == 0:
        return col < reader
    if dr == 1:
        return col >= 0
    return col >= reader - 1


def kernel(
    dp_size, group, q_ref, k_ref, v_ref, do_ref, bias_ref, len_ref, freq_ref,
    att_ref, gq_ref, gk_ref, gv_ref, bg_ref,
    kbuf, vbuf, qs, dos, s_ref, w_ref, mx_ref, acc_ref, stat_ref,
    gkb, gvb, far_k, far_v, nl_k, nl_v, nr_k, nr_v, rz_k, rz_v, zs_k, zs_v, sp_k, sp_v,
    acck, accv, bst, cos_ref, sin_ref, start_ref,
    send_sems, krecv, vrecv, rrecv, brecv,
):
    c = lax.axis_index("ctx")
    d = lax.axis_index("dp")
    x = lax.rem(c, SIDE)
    z = lax.div(c, SIDE)
    base = z * SIDE
    xr, xl, xo = lax.rem(x + 1, SIDE), lax.rem(x + 3, SIDE), lax.rem(x + 2, SIDE)
    right, left = base + xr, base + xl
    scale = 1.0 / math.sqrt(HD)
    heads = 2 * group
    special_from, special_to = c == 3, c == 12

    barrier = pltpu.get_barrier_semaphore()
    stages = [("ctx", 1, SIDE), ("ctx", SIDE, SIDE)]
    stages += [("dp", stride, size) for stride, size in dp_stages(dp_size)]

    def peer(axis, stride, size, step):
        me = c if axis == "ctx" else d
        at = lax.rem(lax.div(me, stride), size)
        other = lax.rem(at + step, size)
        return me + (other - at) * stride, at, other

    count = 0
    for axis, stride, size in stages:
        for step in range(1, size):
            target, _, _ = peer(axis, stride, size, step)
            pl.semaphore_signal(barrier, inc=1, device_id={axis: target}, device_id_type=MESH)
            count += 1

    @pl.when(special_from)
    def _():
        pl.semaphore_signal(barrier, inc=1, device_id={"ctx": c + 9}, device_id_type=MESH)

    @pl.when(special_to)
    def _():
        pl.semaphore_signal(barrier, inc=1, device_id={"ctx": c - 9}, device_id_type=MESH)

    pl.semaphore_wait(barrier, count + jnp.where(special_from | special_to, 1, 0))

    pending = []

    def slot(buf, s, blocks=1):
        return buf.at[pl.ds(pl.multiple_of(s * ROWS, ROWS), blocks * ROWS)]

    def send(pred, src, dst, recv_sem, target, axis="ctx"):
        copy = pltpu.make_async_remote_copy(
            src_ref=src, dst_ref=dst, send_sem=send_sems.at[len(pending)], recv_sem=recv_sem,
            device_id={axis: target}, device_id_type=MESH,
        )
        pending.append((pred, copy))

        @pl.when(pred)
        def _():
            copy.start()

    def arrived(pred, dst, recv_sem):
        copy = pltpu.make_async_remote_copy(
            src_ref=dst, dst_ref=dst, send_sem=send_sems.at[0], recv_sem=recv_sem,
            device_id={"ctx": right}, device_id_type=MESH,
        )

        @pl.when(pred)
        def _():
            copy.wait_recv()

    def first(dr):
        return 9 - SIDE * dr

    def own_send(buf, recv, is_key):
        own = slot(buf, 9 + x)
        sem = recv.at[9 + x]
        far = need(0, xo, x)
        to_right, to_left = need(0, xr, x), need(0, xl, x)
        send(z < 3, own, slot(buf, 5 + x), recv.at[5 + x], c + 4)
        send(z < 2, own, slot(buf, 1 + x), recv.at[1 + x], c + 8)
        send(to_right | far if is_key else to_right, own, own, sem, right)
        send(to_left if is_key else to_left | far, own, own, sem, left)
        send(special_from, own, slot(buf, 0), recv.at[0], c + 9)

    def relay(buf, recv, is_key, dr):
        valid = z >= dr
        s = first(dr) + x
        own, sem = slot(buf, s), recv.at[s]
        arrived(valid, own, sem)
        far = need(dr, xo, x)
        to_right, to_left = need(dr, xr, x), need(dr, xl, x)
        send(valid & (to_right | far if is_key else to_right), own, own, sem, right)
        send(valid & (to_left if is_key else to_left | far), own, own, sem, left)

    def forward(dr):
        valid = z >= dr
        sl, sr = first(dr) + xl, first(dr) + xr
        kl, kr, vl, vr = slot(kbuf, sl), slot(kbuf, sr), slot(vbuf, sl), slot(vbuf, sr)
        arrived(valid & (need(dr, x, xl) | need(dr, xr, xl)), kl, krecv.at[sl])
        send(valid & need(dr, xr, xl), kl, kl, krecv.at[sl], right)
        arrived(valid & (need(dr, x, xr) | need(dr, xl, xr)), vr, vrecv.at[sr])
        send(valid & need(dr, xl, xr), vr, vr, vrecv.at[sr], left)
        arrived(valid & need(dr, x, xr), kr, krecv.at[sr])
        arrived(valid & need(dr, x, xl), vl, vrecv.at[sl])

    def last(dr):
        valid = z >= dr
        so = first(dr) + xo
        arrived(valid & need(dr, x, xo), slot(kbuf, so), krecv.at[so])
        arrived(valid & need(dr, x, xo), slot(vbuf, so), vrecv.at[so])

    vbuf[pl.ds(pl.multiple_of((9 + x) * ROWS, ROWS), ROWS), :] = v_ref[...]
    own_send(vbuf, vrecv, False)

    pos = c * ROWS + lax.broadcasted_iota(jnp.int32, (ROWS, HD), 0)
    start = jnp.zeros((ROWS, HD), jnp.int32)
    end = jnp.int32(0)
    for i in range(len_ref.shape[1]):
        length = len_ref[0, i]
        end = end + length
        start = start + jnp.where(end <= pos, length, 0)
    start_ref[...] = start
    angle = (pos - start).astype(F32) * freq_ref[...]
    lane = lax.broadcasted_iota(jnp.int32, (ROWS, HD), 1)
    cos_ref[...] = jnp.cos(angle)
    sine = jnp.sin(angle)
    sin_ref[...] = jnp.where(lane < HD // 2, -sine, sine)

    def rope(value):
        return value * cos_ref[...] + pltpu.roll(value, HD // 2, 1) * sin_ref[...]

    def rope_back(value):
        return value * cos_ref[...] - pltpu.roll(value, HD // 2, 1) * sin_ref[...]

    own_rows = pl.ds(pl.multiple_of((9 + x) * ROWS, ROWS), ROWS)
    for g in range(2):
        cols = slice(g * HD, (g + 1) * HD)
        kbuf[own_rows, cols] = rope(k_ref[:, cols].astype(F32)).astype(BF16)
    own_send(kbuf, krecv, True)

    def clear(s):
        rows = pl.ds(pl.multiple_of(s * ROWS, ROWS), ROWS)
        kbuf[rows, :] = jnp.zeros((ROWS, 2 * HD), BF16)
        vbuf[rows, :] = jnp.zeros((ROWS, 2 * HD), BF16)

    for dr in (1, 2):

        @pl.when(z < dr)
        def _():
            for i in range(SIDE):
                clear(jnp.int32(first(dr) + i))

    @pl.when(c != 12)
    def _():
        clear(jnp.int32(0))

    @pl.when(x == 0)
    def _():
        gvb[10 * ROWS : 11 * ROWS, :] = jnp.zeros((ROWS, 2 * HD), BF16)

    for h in range(heads):
        g, r = h // group, (h % group) * ROWS
        cols = slice(h * HD, (h + 1) * HD)
        qs[g, r : r + ROWS, :] = rope(q_ref[:, cols].astype(F32) + bias_ref[:, cols]).astype(BF16)
        dos[g, r : r + ROWS, :] = do_ref[:, cols]

    for dr in (1, 2):
        relay(vbuf, vrecv, False, dr)
        relay(kbuf, krecv, True, dr)
    for dr in (0, 1, 2):
        forward(dr)
    for dr in (0, 1, 2):
        last(dr)
    arrived(special_to, slot(kbuf, 0), krecv.at[0])
    arrived(special_to, slot(vbuf, 0), vrecv.at[0])

    nt = (((1,), (1,)), ((), ()))
    tn = (((0,), (0,)), ((), ()))
    nn = (((1,), (0,)), ((), ()))

    def window(p):
        return pl.ds(pl.multiple_of((x + 2 * p) * ROWS, ROWS), 2 * ROWS)

    first_key = (c - (WINDOW - 1)) * ROWS

    for g in range(2):
        mx_ref[g] = jnp.full((group * ROWS, HD), FILL, F32)

    def score_step(p, carry):
        key_pos = first_key + p * 2 * ROWS + lax.broadcasted_iota(jnp.int32, (ROWS, 2 * ROWS), 1)
        row = c * ROWS + lax.broadcasted_iota(jnp.int32, (ROWS, 2 * ROWS), 0)
        begin = jnp.concatenate([start_ref[...], start_ref[...]], axis=1)
        visible = (key_pos <= row) & (key_pos >= begin)
        for g in range(2):
            keys = kbuf[window(p), g * HD : (g + 1) * HD]
            raw = lax.dot_general(qs[g], keys, nt, preferred_element_type=F32)
            for h in range(group):
                rows = slice(h * ROWS, (h + 1) * ROWS)
                part = jnp.where(visible, raw[rows], FILL)
                s_ref[g, p, rows] = part
                mx_ref[g, rows] = jnp.maximum(
                    mx_ref[g, rows], jnp.maximum(part[:, :HD], part[:, HD:])
                )
        return carry

    lax.fori_loop(0, PAIRS, score_step, 0)

    factor = scale * math.log2(math.e)

    for g in range(2):
        for h in range(group):
            rows = slice(h * ROWS, (h + 1) * ROWS)
            top = jnp.max(mx_ref[g, rows], axis=1, keepdims=True)
            mx_ref[g, rows] = jnp.broadcast_to(top, (ROWS, HD))
        acc_ref[g] = jnp.zeros((group * ROWS, HD), F32)

    def exp_step(p, carry):
        for g in range(2):
            for h in range(group):
                rows = slice(h * ROWS, (h + 1) * ROWS)
                top = mx_ref[g, rows]
                lo = jnp.exp2((s_ref[g, p, rows, :HD] - top) * factor)
                hi = jnp.exp2((s_ref[g, p, rows, HD:] - top) * factor)
                s_ref[g, p, rows, :HD] = lo
                s_ref[g, p, rows, HD:] = hi
                acc_ref[g, rows] += lo + hi
        return carry

    lax.fori_loop(0, PAIRS, exp_step, 0)

    for g in range(2):
        for h in range(group):
            rows = slice(h * ROWS, (h + 1) * ROWS)
            total = jnp.sum(acc_ref[g, rows], axis=1, keepdims=True)
            stat_ref[g, rows] = jnp.broadcast_to(1.0 / total, (ROWS, HD))
        acc_ref[g] = jnp.zeros((group * ROWS, HD), F32)

    def out_step(p, carry):
        for g in range(2):
            inverse = stat_ref[g]
            lo = (s_ref[g, p, :, :HD] * inverse).astype(BF16)
            hi = (s_ref[g, p, :, HD:] * inverse).astype(BF16)
            weights = jnp.concatenate([lo, hi], axis=1)
            w_ref[g, p] = weights
            values = vbuf[window(p), g * HD : (g + 1) * HD]
            acc_ref[g] += lax.dot_general(weights, values, nn, preferred_element_type=F32)
        return carry

    lax.fori_loop(0, PAIRS, out_step, 0)

    for g in range(2):
        for h in range(group):
            rows = slice(h * ROWS, (h + 1) * ROWS)
            attended = acc_ref[g, rows].astype(BF16)
            at = (g * group + h) * HD
            att_ref[:, at : at + HD] = attended
            delta = jnp.sum(
                dos[g, rows].astype(F32) * attended.astype(F32), axis=1, keepdims=True
            )
            stat_ref[g, rows] = jnp.broadcast_to(delta, (ROWS, HD))
        acc_ref[g] = jnp.zeros((group * ROWS, HD), F32)

    def grad_step(p, carry):
        for g in range(2):
            cols = slice(g * HD, (g + 1) * HD)
            keys, values = kbuf[window(p), cols], vbuf[window(p), cols]
            prob = lax.dot_general(dos[g], values, nt, preferred_element_type=F32)
            delta = stat_ref[g]
            weights = w_ref[g, p]
            lo = weights[:, :HD].astype(F32) * (prob[:, :HD] - delta)
            hi = weights[:, HD:].astype(F32) * (prob[:, HD:] - delta)
            dscore = jnp.concatenate([lo.astype(BF16), hi.astype(BF16)], axis=1)
            acc_ref[g] += lax.dot_general(dscore, keys, nn, preferred_element_type=F32)
            key_term = lax.dot_general(dscore, qs[g], tn, preferred_element_type=F32)
            value_term = lax.dot_general(weights, dos[g], tn, preferred_element_type=F32)
            gkb[window(p), cols] = (scale * key_term).astype(BF16)
            gvb[window(p), cols] = value_term.astype(BF16)
        return carry

    def back_far(dr):
        so = first(dr) + xo
        pred = (z >= dr) & need(dr, x, xo)
        send(pred, slot(gkb, so), far_k.at[dr], rrecv.at[dr, 0], left)
        send(pred, slot(gvb, so), far_v.at[dr], rrecv.at[dr, 1], right)

    def add_into(buf, s, other):
        rows = pl.ds(pl.multiple_of(s * ROWS, ROWS), ROWS)
        buf[rows, :] = (buf[rows, :].astype(F32) + other[...].astype(F32)).astype(BF16)

    def back_near(dr):
        valid = z >= dr
        sl, sr = first(dr) + xl, first(dr) + xr
        send(valid & need(dr, x, xl), slot(gvb, sl), nr_v.at[dr], rrecv.at[dr, 3], left)
        send(valid & need(dr, x, xr), slot(gkb, sr), nl_k.at[dr], rrecv.at[dr, 4], right)
        got = valid & need(dr, xr, xl)
        arrived(got, far_k.at[dr], rrecv.at[dr, 0])

        @pl.when(got)
        def _():
            add_into(gkb, sl, far_k.at[dr])

        pred = valid & (need(dr, x, xl) | need(dr, xr, xl))
        send(pred, slot(gkb, sl), nr_k.at[dr], rrecv.at[dr, 2], left)
        got_v = valid & need(dr, xl, xr)
        arrived(got_v, far_v.at[dr], rrecv.at[dr, 1])

        @pl.when(got_v)
        def _():
            add_into(gvb, sr, far_v.at[dr])

        pred = valid & (need(dr, x, xr) | need(dr, xl, xr))
        send(pred, slot(gvb, sr), nl_v.at[dr], rrecv.at[dr, 5], right)

    def add_when(pred, acc, src, sem):
        arrived(pred, src, sem)

        @pl.when(pred)
        def _():
            acc[...] += src[...].astype(F32)

    def back_sum(dr):
        valid = z >= dr
        so = pl.ds(pl.multiple_of((first(dr) + x) * ROWS, ROWS), ROWS)
        acck[...] = gkb[so, :].astype(F32)
        accv[...] = gvb[so, :].astype(F32)
        near_l, near_r, far = need(dr, xl, x), need(dr, xr, x), need(dr, xo, x)
        add_when(valid & near_r, accv, nr_v.at[dr], rrecv.at[dr, 3])
        add_when(valid & near_l, acck, nl_k.at[dr], rrecv.at[dr, 4])
        add_when(valid & (near_r | far), acck, nr_k.at[dr], rrecv.at[dr, 2])
        add_when(valid & (near_l | far), accv, nl_v.at[dr], rrecv.at[dr, 5])
        if dr:
            zs_k[dr - 1] = acck[...].astype(BF16)
            zs_v[dr - 1] = accv[...].astype(BF16)
            down = c - SIDE * dr
            send(valid, zs_k.at[dr - 1], rz_k.at[dr - 1], rrecv.at[dr, 6], down)
            send(valid, zs_v.at[dr - 1], rz_v.at[dr - 1], rrecv.at[dr, 7], down)

    lax.fori_loop(0, 3, grad_step, 0)
    back_far(2)
    send(special_to, slot(gkb, 0), sp_k, rrecv.at[0, 6], c - 9)
    send(special_to, slot(gvb, 0), sp_v, rrecv.at[0, 7], c - 9)
    back_near(2)
    lax.fori_loop(3, PAIRS, grad_step, 0)
    back_far(1)
    back_far(0)
    back_near(1)
    back_near(0)
    back_sum(2)

    for h in range(heads):
        g, r = h // group, (h % group) * ROWS
        cols = slice(h * HD, (h + 1) * HD)
        before = rope_back(scale * acc_ref[g, r : r + ROWS])
        gq_ref[:, cols] = before.astype(BF16)
        bst[0, x, h : h + 1, :] = jnp.sum(before, axis=0, keepdims=True)
    pad = bst.shape[2] - heads
    if pad:
        bst[0, x, heads:, :] = jnp.zeros((pad, HD), F32)

    def bias_start(i):
        axis, stride, size = stages[i]
        for step in range(1, size):
            target, at, _ = peer(axis, stride, size, step)
            send(c >= 0, bst.at[i, at], bst.at[i, at], brecv.at[i, at], target, axis)

    def bias_end(i):
        axis, stride, size = stages[i]
        for step in range(1, size):
            _, _, other = peer(axis, stride, size, step)
            arrived(c >= 0, bst.at[i, other], brecv.at[i, other])
        total = bst[i, 0]
        for j in range(1, size):
            total = total + bst[i, j]
        if i + 1 < len(stages):
            axis, stride, size = stages[i + 1]
            _, at, _ = peer(axis, stride, size, 1)
            bst[i + 1, at] = total
            bias_start(i + 1)
        else:
            total = total * (1.0 / math.sqrt(dp_size * SIDE * SIDE * ROWS))
            for h in range(heads):
                bg_ref[:, h * HD : (h + 1) * HD] = total[h : h + 1]

    bias_start(0)
    back_sum(1)
    bias_end(0)
    back_sum(0)
    bias_end(1)
    for dr in (2, 1):
        add_when(z + dr < SIDE, acck, rz_k.at[dr - 1], rrecv.at[dr, 6])
        add_when(z + dr < SIDE, accv, rz_v.at[dr - 1], rrecv.at[dr, 7])
    add_when(special_from, acck, sp_k, rrecv.at[0, 6])
    add_when(special_from, accv, sp_v, rrecv.at[0, 7])
    for g in range(2):
        cols = slice(g * HD, (g + 1) * HD)
        gk_ref[:, cols] = rope_back(acck[:, cols]).astype(BF16)
    gv_ref[...] = accv[...].astype(BF16)
    for i in range(2, len(stages)):
        bias_end(i)

    for pred, copy in pending:

        @pl.when(pred)
        def _():
            copy.wait_send()


def shards(q_lin, k_lin, v_lin, out_grad, q_bias, doc_lengths):
    width = q_lin.shape[2]
    heads = width // HD
    group = heads // 2
    dp_size = lax.axis_size("dp")
    exponent = np.arange(HD // 2, dtype=np.float32) * np.float32(2.0 / HD)
    freq = np.power(np.float32(THETA), -exponent).astype(np.float32)
    freq = jnp.asarray(np.concatenate([freq, freq])[None, :])
    rows = group * ROWS
    vmem = pl.BlockSpec(memory_space=pltpu.VMEM)
    block = lambda *lead: pltpu.VMEM((*lead, ROWS, 2 * HD), BF16)
    n_stage = 2 + len(dp_stages(dp_size))
    pad_heads = -(-heads // 8) * 8
    outs = pl.pallas_call(
        lambda *refs: kernel(dp_size, group, *refs),
        out_shape=(
            jax.ShapeDtypeStruct((ROWS, width), BF16),
            jax.ShapeDtypeStruct((ROWS, width), BF16),
            jax.ShapeDtypeStruct((ROWS, 2 * HD), BF16),
            jax.ShapeDtypeStruct((ROWS, 2 * HD), BF16),
            jax.ShapeDtypeStruct((1, width), F32),
        ),
        in_specs=[vmem] * 5 + [pl.BlockSpec(memory_space=pltpu.SMEM), vmem],
        out_specs=(vmem,) * 5,
        scratch_shapes=[
            pltpu.VMEM((SLOTS * ROWS, 2 * HD), BF16),
            pltpu.VMEM((SLOTS * ROWS, 2 * HD), BF16),
            pltpu.VMEM((2, rows, HD), BF16),
            pltpu.VMEM((2, rows, HD), BF16),
            pltpu.VMEM((2, PAIRS, rows, 2 * ROWS), F32),
            pltpu.VMEM((2, PAIRS, rows, 2 * ROWS), BF16),
            pltpu.VMEM((2, rows, HD), F32),
            pltpu.VMEM((2, rows, HD), F32),
            pltpu.VMEM((2, rows, HD), F32),
            pltpu.VMEM((SLOTS * ROWS, 2 * HD), BF16),
            pltpu.VMEM((SLOTS * ROWS, 2 * HD), BF16),
            block(3), block(3), block(3), block(3), block(3), block(3),
            block(2), block(2), block(2), block(2), block(), block(),
            pltpu.VMEM((ROWS, 2 * HD), F32),
            pltpu.VMEM((ROWS, 2 * HD), F32),
            pltpu.VMEM((n_stage, SIDE, pad_heads, HD), F32),
            pltpu.VMEM((ROWS, HD), F32),
            pltpu.VMEM((ROWS, HD), F32),
            pltpu.VMEM((ROWS, HD), jnp.int32),
            pltpu.SemaphoreType.DMA((72,)),
            pltpu.SemaphoreType.DMA((SLOTS,)),
            pltpu.SemaphoreType.DMA((SLOTS,)),
            pltpu.SemaphoreType.DMA((3, 8)),
            pltpu.SemaphoreType.DMA((n_stage, SIDE)),
        ],
        compiler_params=pltpu.CompilerParams(
            collective_id=0, has_side_effects=True, vmem_limit_bytes=56 * 1024 * 1024
        ),
        cost_estimate=pl.CostEstimate(
            flops=12 * heads * ROWS * WINDOW * ROWS * HD,
            bytes_accessed=4 * 2 * ROWS * width,
            transcendentals=heads * ROWS * WINDOW * ROWS,
        ),
    )(
        q_lin.reshape(ROWS, width), k_lin.reshape(ROWS, 2 * HD), v_lin.reshape(ROWS, 2 * HD),
        out_grad.reshape(ROWS, width), q_bias.reshape(1, width), doc_lengths, freq,
    )
    attended, grad_q, grad_k, grad_v, bias_grad = outs
    return (attended[None], grad_q[None], grad_k[None], grad_v[None], bias_grad.reshape(width))


def solution(mesh):
    rows = P("dp", "ctx", None)
    return jax.shard_map(
        shards,
        mesh=mesh,
        in_specs=(rows, rows, rows, rows, P(), P("dp", None)),
        out_specs=(rows, rows, rows, rows, P()),
        check_vma=False,
    )
```

time: 411 us -> 87.2 us (0.21)
  the two profiles are of different devices: /device:TPU:16 before, /device:TPU:1 now
where the time goes in v1:
time: 87.2 us; the launch traced here: 86.9 us
  Pallas kernels  79.4 us (91%)
  local copies, waits for them, and re-layouts  6.21 us (7%)
    pallas_call x1, Pallas kernels, shards(): pl.pallas_call(lambda *refs: kernel(dp_size, group, *refs), out_shape=(ja...  79.4 us
    unnamed x12, local copies, waits for them, and re-layouts  4.91 us

profile of v1, /device:TPU:1, one launch (start us, length us, event | category | flops | bytes accessed | tf_op | source)
XLA Modules:
  0.0 86.9 jit_solution(10573563851348096611)
XLA Ops:
  0.6 1.3 %reshape.32.refs_4_ = f32[1,1792]{1,0:T(1,128)} reshape(f32[1792]{0:T(1024)} %param.11) | data formatting | bytes 14336 | tf_op jit(solution)/shard_map/reshape | solution.py:507
  1.9 79.4 %shard_map.110 = (bf16[128,1792]{1,0:T(8,128)(2,1)}, bf16[128,1792]{1,0:T(8,128)(2,1)}, bf16[128,256]{1,0:T(8,128)(2,1)}, bf16[128,256]{1,0:T(8,128)(2,1)}, f32[1,1792]{1,0:T(1,128)}) custom-call(bf16[128,1792]{1,0:T(8,128)(2,1)} %bitcast.12, bf16[128,256]{1,0:T(8,128)(2,1)} %bitcast.14, bf16[128,256]{1,0:T(8,128)(2,1)} %bitcast.15, ...), custom_call_target="tpu_custom_call" | custom-call | flops 3523215360 | bytes 1835008 | tf_op jit(solution)/shard_map/pallas_call | solution.py:460
  81.3 0.0 copy-start.3
  81.4 0.7 copy-done.3
  82.0 0.6 reduce
  82.7 0.0 copy-start
  82.7 1.9 %copy.16 = bf16[1,128,1792]{2,1,0:T(8,128)(2,1)} copy(bf16[1,128,1792]{2,1,0:T(8,128)(2,1)} %bitcast.9) | data formatting | bytes 917504
  84.5 0.0 copy-done
  84.5 0.0 copy-start.2
  84.5 0.8 copy.17
  85.3 0.1 copy-done.2
  85.4 0.0 copy-start.1
  85.4 0.6 copy.18
  86.0 0.2 copy-done.1
  86.3 0.6 copy.19
Async XLA Ops:
  81.3 0.7 copy-start.3
  82.7 1.9 %copy-start = (bf16[128,1792]{1,0:T(8,128)(2,1)S(1)}, bf16[128,1792]{1,0:T(8,128)(2,1)}, u32[]{:S(2)}) copy-start(bf16[128,1792]{1,0:T(8,128)(2,1)} %get-tuple-element.11) | copy-start | bytes 1376260
  84.5 0.9 copy-start.2
  85.4 0.9 copy-start.1

commit v2 on v1

v2 whole, which is shorter than its diff:
```python
import math

import jax
import jax.numpy as jnp
import numpy as np
from jax import lax
from jax.experimental import pallas as pl
from jax.experimental.pallas import tpu as pltpu
from jax.sharding import PartitionSpec as P

HD = 128
ROWS = 128
SIDE = 4
WINDOW = 10
SLOTS = 13
PAIRS = WINDOW // 2
THETA = 1000000.0
FILL = -1e30
MESH = pl.DeviceIdType.MESH
F32 = jnp.float32
BF16 = jnp.bfloat16


def bias_stages(dp_size):
    if dp_size == 32:
        return [("z", 4 * SIDE), ("x", SIDE), ("yc", 2 * SIDE)]
    return [("z", SIDE), ("x", SIDE)]


def need(dr, reader, col):
    if dr == 0:
        return col < reader
    if dr == 1:
        return col >= 0
    return col >= reader - 1


def kernel(
    dp_size, group, q_hbm, k_hbm, v_hbm, do_hbm, bias_ref, len_ref, freq_ref,
    att_hbm, gq_hbm, gk_hbm, gv_hbm, bg_ref,
    q_ref, k_ref, v_ref, do_ref, att_ref, gq_ref, gk_ref, gv_ref,
    kbuf, vbuf, qs, dos, s_ref, p_ref, w_ref, ds_ref, mx_ref, acc_ref, stat_ref,
    gkb, gvb, far_k, far_v, nl_k, nl_v, nr_k, nr_v, rz_k, rz_v, zs_k, zs_v, sp_k, sp_v,
    acck, accv, bst, cos_ref, sin_ref, start_ref,
    send_sems, krecv, vrecv, rrecv, brecv, local_sems,
):
    c = lax.axis_index("ctx")
    d = lax.axis_index("dp")
    x = lax.rem(c, SIDE)
    z = lax.div(c, SIDE)
    base = z * SIDE
    xr, xl, xo = lax.rem(x + 1, SIDE), lax.rem(x + 3, SIDE), lax.rem(x + 2, SIDE)
    right, left = base + xr, base + xl
    scale = 1.0 / math.sqrt(HD)
    heads = 2 * group
    special_from, special_to = c == 3, c == 12

    def load(src, dst, i):
        pltpu.make_async_copy(src, dst, local_sems.at[i]).start()

    def loaded(src, dst, i):
        pltpu.make_async_copy(src, dst, local_sems.at[i]).wait()

    barrier = pltpu.get_barrier_semaphore()
    stages = bias_stages(dp_size)

    def peer(kind, size, step):
        if kind == "x":
            other = lax.rem(x + step, SIDE)
            return {"ctx": base + other}, x, other
        if kind == "z":
            high = lax.rem(lax.div(d, 2), SIDE) if size > SIDE else 0
            at = high * SIDE + z
            other = lax.rem(at + step, size)
            ctx = lax.rem(other, SIDE) * SIDE + x
            return {"dp": d + (lax.div(other, SIDE) - high) * 2, "ctx": ctx}, at, other
        y, core = lax.div(d, 8), lax.rem(d, 2)
        at = y * 2 + core
        other = lax.rem(at + step, size)
        move = (lax.div(other, 2) - y) * 8 + lax.rem(other, 2) - core
        return {"dp": d + move}, at, other

    count = jnp.where(special_from | special_to, 1, 0)
    for kind, size in stages:
        for step in range(1, size):
            target, _, _ = peer(kind, size, step)
            pl.semaphore_signal(barrier, inc=1, device_id=target, device_id_type=MESH)
        count = count + (size - 1)

    @pl.when(special_from)
    def _():
        pl.semaphore_signal(barrier, inc=1, device_id={"ctx": c + 9}, device_id_type=MESH)

    @pl.when(special_to)
    def _():
        pl.semaphore_signal(barrier, inc=1, device_id={"ctx": c - 9}, device_id_type=MESH)

    load(q_hbm, q_ref, 0)
    load(do_hbm, do_ref, 1)
    load(k_hbm, k_ref, 2)
    load(v_hbm, v_ref, 3)
    pl.semaphore_wait(barrier, count)

    pending = []

    def slot(buf, s, blocks=1):
        return buf.at[pl.ds(pl.multiple_of(s * ROWS, ROWS), blocks * ROWS)]

    def send(pred, src, dst, recv_sem, target):
        target = target if isinstance(target, dict) else {"ctx": target}
        copy = pltpu.make_async_remote_copy(
            src_ref=src, dst_ref=dst, send_sem=send_sems.at[len(pending)], recv_sem=recv_sem,
            device_id=target, device_id_type=MESH,
        )
        pending.append((pred, copy))

        @pl.when(pred)
        def _():
            copy.start()

    def arrived(pred, dst, recv_sem):
        copy = pltpu.make_async_remote_copy(
            src_ref=dst, dst_ref=dst, send_sem=send_sems.at[0], recv_sem=recv_sem,
            device_id={"ctx": right}, device_id_type=MESH,
        )

        @pl.when(pred)
        def _():
            copy.wait_recv()

    def first(dr):
        return 9 - SIDE * dr

    def far_path(dr):
        return dr != 2

    def spread(buf, recv, is_key, dr):
        valid = z >= dr
        s = first(dr) + x
        own, sem = slot(buf, s), recv.at[s]
        if dr:
            arrived(valid, own, sem)
        if dr < 2:
            up = slot(buf, s - SIDE)
            send(valid & (z < SIDE - 1), own, up, recv.at[s - SIDE], c + SIDE)
        far = need(dr, xo, x)
        if not far_path(dr):
            send(valid & far, own, own, sem, base + xo)
        to_right, to_left = need(dr, xr, x), need(dr, xl, x)
        on_right, on_left = far_path(dr) & is_key, far_path(dr) & (not is_key)
        send(valid & (to_right | far if on_right else to_right), own, own, sem, right)
        send(valid & (to_left | far if on_left else to_left), own, own, sem, left)
        if dr == 0:
            send(special_from, own, slot(buf, 0), recv.at[0], c + 9)

    def forward(dr):
        valid = z >= dr
        sl, sr = first(dr) + xl, first(dr) + xr
        kl, kr, vl, vr = slot(kbuf, sl), slot(kbuf, sr), slot(vbuf, sl), slot(vbuf, sr)
        use_l, use_r = need(dr, x, xl), need(dr, x, xr)
        if far_path(dr):
            on_v, on_k = need(dr, xl, xr), need(dr, xr, xl)
            arrived(valid & (use_r | on_v), vr, vrecv.at[sr])
            send(valid & on_v, vr, vr, vrecv.at[sr], left)
            arrived(valid & (use_l | on_k), kl, krecv.at[sl])
            send(valid & on_k, kl, kl, krecv.at[sl], right)
        else:
            arrived(valid & use_r, vr, vrecv.at[sr])
            arrived(valid & use_l, kl, krecv.at[sl])
        arrived(valid & use_l, vl, vrecv.at[sl])
        arrived(valid & use_r, kr, krecv.at[sr])

    def last(dr):
        valid = z >= dr
        so = first(dr) + xo
        arrived(valid & need(dr, x, xo), slot(kbuf, so), krecv.at[so])
        arrived(valid & need(dr, x, xo), slot(vbuf, so), vrecv.at[so])

    loaded(v_hbm, v_ref, 3)
    vbuf[pl.ds(pl.multiple_of((9 + x) * ROWS, ROWS), ROWS), :] = v_ref[...]
    spread(vbuf, vrecv, False, 0)

    pos = c * ROWS + lax.broadcasted_iota(jnp.int32, (ROWS, HD), 0)
    start = jnp.zeros((ROWS, HD), jnp.int32)
    end = jnp.int32(0)
    for i in range(len_ref.shape[1]):
        length = len_ref[0, i]
        end = end + length
        start = start + jnp.where(end <= pos, length, 0)
    start_ref[...] = start
    angle = (pos - start).astype(F32) * freq_ref[...]
    lane = lax.broadcasted_iota(jnp.int32, (ROWS, HD), 1)
    cos_ref[...] = jnp.cos(angle)
    sine = jnp.sin(angle)
    sin_ref[...] = jnp.where(lane < HD // 2, -sine, sine)

    def rope(value):
        return value * cos_ref[...] + pltpu.roll(value, HD // 2, 1) * sin_ref[...]

    def rope_back(value):
        return value * cos_ref[...] - pltpu.roll(value, HD // 2, 1) * sin_ref[...]

    loaded(k_hbm, k_ref, 2)
    own_rows = pl.ds(pl.multiple_of((9 + x) * ROWS, ROWS), ROWS)
    for g in range(2):
        cols = slice(g * HD, (g + 1) * HD)
        kbuf[own_rows, cols] = rope(k_ref[:, cols].astype(F32)).astype(BF16)
    spread(kbuf, krecv, True, 0)

    def clear(s):
        rows = pl.ds(pl.multiple_of(s * ROWS, ROWS), ROWS)
        kbuf[rows, :] = jnp.zeros((ROWS, 2 * HD), BF16)
        vbuf[rows, :] = jnp.zeros((ROWS, 2 * HD), BF16)

    for dr in (1, 2):

        @pl.when(z < dr)
        def _():
            for i in range(SIDE):
                clear(jnp.int32(first(dr) + i))

    @pl.when(c != 12)
    def _():
        clear(jnp.int32(0))

    @pl.when(x == 0)
    def _():
        gvb[10 * ROWS : 11 * ROWS, :] = jnp.zeros((ROWS, 2 * HD), BF16)

    loaded(q_hbm, q_ref, 0)
    loaded(do_hbm, do_ref, 1)
    for h in range(heads):
        g, r = h // group, (h % group) * ROWS
        cols = slice(h * HD, (h + 1) * HD)
        qs[g, r : r + ROWS, :] = rope(q_ref[:, cols].astype(F32) + bias_ref[cols]).astype(BF16)
        dos[g, r : r + ROWS, :] = do_ref[:, cols]

    nt = (((1,), (1,)), ((), ()))
    tn = (((0,), (0,)), ((), ()))
    nn = (((1,), (0,)), ((), ()))

    def window(p):
        return pl.ds(pl.multiple_of((x + 2 * p) * ROWS, ROWS), 2 * ROWS)

    first_key = (c - (WINDOW - 1)) * ROWS

    for g in range(2):
        mx_ref[g] = jnp.full((group * ROWS, HD), FILL, F32)

    def score_step(p):
        key_pos = first_key + p * 2 * ROWS + lax.broadcasted_iota(jnp.int32, (ROWS, 2 * ROWS), 1)
        row = c * ROWS + lax.broadcasted_iota(jnp.int32, (ROWS, 2 * ROWS), 0)
        begin = jnp.concatenate([start_ref[...], start_ref[...]], axis=1)
        visible = (key_pos <= row) & (key_pos >= begin)
        for g in range(2):
            keys = kbuf[window(p), g * HD : (g + 1) * HD]
            raw = lax.dot_general(qs[g], keys, nt, preferred_element_type=F32)
            for h in range(group):
                rows = slice(h * ROWS, (h + 1) * ROWS)
                part = jnp.where(visible, raw[rows], FILL)
                s_ref[g, p, rows] = part
                mx_ref[g, rows] = jnp.maximum(
                    mx_ref[g, rows], jnp.maximum(part[:, :HD], part[:, HD:])
                )
            values = vbuf[window(p), g * HD : (g + 1) * HD]
            p_ref[g, p] = lax.dot_general(dos[g], values, nt, preferred_element_type=F32)
        return 0

    spread(vbuf, vrecv, False, 1)
    spread(kbuf, krecv, True, 1)
    forward(0)
    spread(vbuf, vrecv, False, 2)
    spread(kbuf, krecv, True, 2)
    forward(1)
    score_step(4)
    forward(2)
    arrived(special_to, slot(kbuf, 0), krecv.at[0])
    arrived(special_to, slot(vbuf, 0), vrecv.at[0])
    lax.fori_loop(0, 2, lambda i, carry: score_step(2 - 2 * i), 0)
    last(0)
    last(1)
    last(2)
    lax.fori_loop(0, 2, lambda i, carry: score_step(3 - 2 * i), 0)

    factor = scale * math.log2(math.e)

    for g in range(2):
        for h in range(group):
            rows = slice(h * ROWS, (h + 1) * ROWS)
            top = jnp.max(mx_ref[g, rows], axis=1, keepdims=True)
            mx_ref[g, rows] = jnp.broadcast_to(top, (ROWS, HD))
        acc_ref[g] = jnp.zeros((group * ROWS, HD), F32)

    def exp_step(p, carry):
        for g in range(2):
            for h in range(group):
                rows = slice(h * ROWS, (h + 1) * ROWS)
                top = mx_ref[g, rows]
                lo = jnp.exp2((s_ref[g, p, rows, :HD] - top) * factor)
                hi = jnp.exp2((s_ref[g, p, rows, HD:] - top) * factor)
                s_ref[g, p, rows, :HD] = lo
                s_ref[g, p, rows, HD:] = hi
                acc_ref[g, rows] += lo + hi
        return carry

    lax.fori_loop(0, PAIRS, exp_step, 0)

    for g in range(2):
        for h in range(group):
            rows = slice(h * ROWS, (h + 1) * ROWS)
            total = jnp.sum(acc_ref[g, rows], axis=1, keepdims=True)
            stat_ref[g, rows] = jnp.broadcast_to(1.0 / total, (ROWS, HD))
        acc_ref[g] = jnp.zeros((group * ROWS, HD), F32)

    def out_step(p, carry):
        for g in range(2):
            inverse = stat_ref[g]
            lo = (s_ref[g, p, :, :HD] * inverse).astype(BF16)
            hi = (s_ref[g, p, :, HD:] * inverse).astype(BF16)
            weights = jnp.concatenate([lo, hi], axis=1)
            w_ref[g, p] = weights
            values = vbuf[window(p), g * HD : (g + 1) * HD]
            acc_ref[g] += lax.dot_general(weights, values, nn, preferred_element_type=F32)
        return carry

    lax.fori_loop(0, PAIRS, out_step, 0)

    for g in range(2):
        for h in range(group):
            rows = slice(h * ROWS, (h + 1) * ROWS)
            attended = acc_ref[g, rows].astype(BF16)
            at = (g * group + h) * HD
            att_ref[:, at : at + HD] = attended
            delta = jnp.sum(
                dos[g, rows].astype(F32) * attended.astype(F32), axis=1, keepdims=True
            )
            stat_ref[g, rows] = jnp.broadcast_to(delta, (ROWS, HD))
        acc_ref[g] = jnp.zeros((group * ROWS, HD), F32)

    load(att_ref, att_hbm, 4)
    _, at_0, _ = peer(*stages[0], 1)

    def dscore_step(p, carry):
        for g in range(2):
            keys = kbuf[window(p), g * HD : (g + 1) * HD]
            delta = stat_ref[g]
            lo = w_ref[g, p, :, :HD].astype(F32) * (p_ref[g, p, :, :HD] - delta)
            hi = w_ref[g, p, :, HD:].astype(F32) * (p_ref[g, p, :, HD:] - delta)
            dscore = jnp.concatenate([lo.astype(BF16), hi.astype(BF16)], axis=1)
            ds_ref[g, p] = dscore
            acc_ref[g] += lax.dot_general(dscore, keys, nn, preferred_element_type=F32)
        return carry

    lax.fori_loop(0, PAIRS, dscore_step, 0)
    for h in range(heads):
        g, r = h // group, (h % group) * ROWS
        cols = slice(h * HD, (h + 1) * HD)
        before = rope_back(scale * acc_ref[g, r : r + ROWS])
        gq_ref[:, cols] = before.astype(BF16)
        bst[0, at_0, h : h + 1, :] = jnp.sum(before, axis=0, keepdims=True)
    pad = bst.shape[2] - heads
    if pad:
        bst[0, at_0, heads:, :] = jnp.zeros((pad, HD), F32)
    load(gq_ref, gq_hbm, 5)

    def bias_start(i):
        kind, size = stages[i]
        for step in range(1, size):
            target, at, _ = peer(kind, size, step)
            send(c >= 0, bst.at[i, at], bst.at[i, at], brecv.at[i, at], target)

    def bias_end(i):
        kind, size = stages[i]
        for step in range(1, size):
            _, _, other = peer(kind, size, step)
            arrived(c >= 0, bst.at[i, other], brecv.at[i, other])
        total = bst[i, 0]
        for j in range(1, size):
            total = total + bst[i, j]
        if i + 1 < len(stages):
            _, at, _ = peer(*stages[i + 1], 1)
            bst[i + 1, at] = total
            bias_start(i + 1)
        else:
            total = total * (1.0 / math.sqrt(dp_size * SIDE * SIDE * ROWS))
            for h in range(heads):
                bg_ref[h * HD : (h + 1) * HD] = total[h]

    bias_start(0)

    def term_step(p, carry):
        for g in range(2):
            cols = slice(g * HD, (g + 1) * HD)
            key_term = lax.dot_general(ds_ref[g, p], qs[g], tn, preferred_element_type=F32)
            value_term = lax.dot_general(w_ref[g, p], dos[g], tn, preferred_element_type=F32)
            gkb[window(p), cols] = (scale * key_term).astype(BF16)
            gvb[window(p), cols] = value_term.astype(BF16)
        return carry

    def back_far(dr):
        so = first(dr) + xo
        pred = (z >= dr) & need(dr, x, xo)
        to_k, to_v = (left, right) if far_path(dr) else (base + xo, base + xo)
        send(pred, slot(gkb, so), far_k.at[dr], rrecv.at[dr, 0], to_k)
        send(pred, slot(gvb, so), far_v.at[dr], rrecv.at[dr, 1], to_v)

    def add_into(buf, s, other):
        rows = pl.ds(pl.multiple_of(s * ROWS, ROWS), ROWS)
        buf[rows, :] = (buf[rows, :].astype(F32) + other[...].astype(F32)).astype(BF16)

    def back_near(dr):
        valid = z >= dr
        sl, sr = first(dr) + xl, first(dr) + xr
        to_l, to_r = valid & need(dr, x, xl), valid & need(dr, x, xr)
        send(to_l, slot(gvb, sl), nr_v.at[dr], rrecv.at[dr, 3], left)
        send(to_r, slot(gkb, sr), nl_k.at[dr], rrecv.at[dr, 4], right)
        if not far_path(dr):
            send(to_l, slot(gkb, sl), nr_k.at[dr], rrecv.at[dr, 2], left)
            send(to_r, slot(gvb, sr), nl_v.at[dr], rrecv.at[dr, 5], right)
            return
        got = valid & need(dr, xr, xl)
        arrived(got, far_k.at[dr], rrecv.at[dr, 0])

        @pl.when(got)
        def _():
            add_into(gkb, sl, far_k.at[dr])

        send(to_l | got, slot(gkb, sl), nr_k.at[dr], rrecv.at[dr, 2], left)
        got_v = valid & need(dr, xl, xr)
        arrived(got_v, far_v.at[dr], rrecv.at[dr, 1])

        @pl.when(got_v)
        def _():
            add_into(gvb, sr, far_v.at[dr])

        send(to_r | got_v, slot(gvb, sr), nl_v.at[dr], rrecv.at[dr, 5], right)

    def add_when(pred, acc, src, sem):
        arrived(pred, src, sem)

        @pl.when(pred)
        def _():
            acc[...] += src[...].astype(F32)

    def back_sum(dr):
        valid = z >= dr
        so = pl.ds(pl.multiple_of((first(dr) + x) * ROWS, ROWS), ROWS)
        acck[...] = gkb[so, :].astype(F32)
        accv[...] = gvb[so, :].astype(F32)
        near_l, near_r, far = need(dr, xl, x), need(dr, xr, x), need(dr, xo, x)
        add_when(valid & near_r, accv, nr_v.at[dr], rrecv.at[dr, 3])
        add_when(valid & near_l, acck, nl_k.at[dr], rrecv.at[dr, 4])
        passed = far & far_path(dr)
        add_when(valid & (near_r | passed), acck, nr_k.at[dr], rrecv.at[dr, 2])
        add_when(valid & (near_l | passed), accv, nl_v.at[dr], rrecv.at[dr, 5])
        if not far_path(dr):
            add_when(valid & far, acck, far_k.at[dr], rrecv.at[dr, 0])
            add_when(valid & far, accv, far_v.at[dr], rrecv.at[dr, 1])
        if dr:
            zs_k[dr - 1] = acck[...].astype(BF16)
            zs_v[dr - 1] = accv[...].astype(BF16)
            down = c - SIDE * dr
            send(valid, zs_k.at[dr - 1], rz_k.at[dr - 1], rrecv.at[dr, 6], down)
            send(valid, zs_v.at[dr - 1], rz_v.at[dr - 1], rrecv.at[dr, 7], down)

    begin_pair = jnp.where(x < 2, 2, 1)
    lax.fori_loop(0, 3, lambda i, carry: term_step(begin_pair + i, carry), 0)
    back_far(1)
    end_pair = jnp.where(x < 2, 1, PAIRS - 1)
    lax.fori_loop(0, 2, lambda i, carry: term_step(i * end_pair, carry), 0)
    back_far(0)
    back_far(2)
    back_near(2)
    send(special_to, slot(gkb, 0), sp_k, rrecv.at[0, 6], c - 9)
    send(special_to, slot(gvb, 0), sp_v, rrecv.at[0, 7], c - 9)
    back_near(1)
    bias_end(0)
    back_near(0)
    back_sum(2)
    if len(stages) > 2:
        bias_end(1)
    back_sum(1)
    back_sum(0)
    for dr in (2, 1):
        add_when(z + dr < SIDE, acck, rz_k.at[dr - 1], rrecv.at[dr, 6])
        add_when(z + dr < SIDE, accv, rz_v.at[dr - 1], rrecv.at[dr, 7])
    add_when(special_from, acck, sp_k, rrecv.at[0, 6])
    add_when(special_from, accv, sp_v, rrecv.at[0, 7])
    for g in range(2):
        cols = slice(g * HD, (g + 1) * HD)
        gk_ref[:, cols] = rope_back(acck[:, cols]).astype(BF16)
    gv_ref[...] = accv[...].astype(BF16)
    load(gk_ref, gk_hbm, 6)
    load(gv_ref, gv_hbm, 7)
    bias_end(len(stages) - 1)
    loaded(att_ref, att_hbm, 4)
    loaded(gq_ref, gq_hbm, 5)
    loaded(gk_ref, gk_hbm, 6)
    loaded(gv_ref, gv_hbm, 7)

    for pred, copy in pending:

        @pl.when(pred)
        def _():
            copy.wait_send()


def write_out(*refs):
    sems = refs[-1]
    copies = [pltpu.make_async_copy(refs[i], refs[5 + i], sems.at[i]) for i in range(5)]
    for copy in copies:
        copy.start()
    for copy in copies:
        copy.wait()


def shards(q_lin, k_lin, v_lin, out_grad, q_bias, doc_lengths):
    width = q_lin.shape[2]
    heads = width // HD
    group = heads // 2
    dp_size = lax.axis_size("dp")
    exponent = np.arange(HD // 2, dtype=np.float32) * np.float32(2.0 / HD)
    freq = np.power(np.float32(THETA), -exponent).astype(np.float32)
    freq = jnp.asarray(np.concatenate([freq, freq])[None, :])
    rows = group * ROWS
    anywhere = pl.BlockSpec(memory_space=pl.ANY)
    vmem = pl.BlockSpec(memory_space=pltpu.VMEM)
    block = lambda *lead: pltpu.VMEM((*lead, ROWS, 2 * HD), BF16)
    n_stage = len(bias_stages(dp_size))
    pad_heads = -(-heads // 8) * 8
    outs = pl.pallas_call(
        lambda *refs: kernel(dp_size, group, *refs),
        out_shape=(
            jax.ShapeDtypeStruct((ROWS, width), BF16),
            jax.ShapeDtypeStruct((ROWS, width), BF16),
            jax.ShapeDtypeStruct((ROWS, 2 * HD), BF16),
            jax.ShapeDtypeStruct((ROWS, 2 * HD), BF16),
            jax.ShapeDtypeStruct((width,), F32),
        ),
        in_specs=[anywhere] * 4 + [vmem, pl.BlockSpec(memory_space=pltpu.SMEM), vmem],
        out_specs=(anywhere,) * 4 + (vmem,),
        scratch_shapes=[
            pltpu.VMEM((ROWS, width), BF16), block(), block(), pltpu.VMEM((ROWS, width), BF16),
            pltpu.VMEM((ROWS, width), BF16), pltpu.VMEM((ROWS, width), BF16), block(), block(),
            pltpu.VMEM((SLOTS * ROWS, 2 * HD), BF16),
            pltpu.VMEM((SLOTS * ROWS, 2 * HD), BF16),
            pltpu.VMEM((2, rows, HD), BF16),
            pltpu.VMEM((2, rows, HD), BF16),
            pltpu.VMEM((2, PAIRS, rows, 2 * ROWS), F32),
            pltpu.VMEM((2, PAIRS, rows, 2 * ROWS), F32),
            pltpu.VMEM((2, PAIRS, rows, 2 * ROWS), BF16),
            pltpu.VMEM((2, PAIRS, rows, 2 * ROWS), BF16),
            pltpu.VMEM((2, rows, HD), F32),
            pltpu.VMEM((2, rows, HD), F32),
            pltpu.VMEM((2, rows, HD), F32),
            pltpu.VMEM((SLOTS * ROWS, 2 * HD), BF16),
            pltpu.VMEM((SLOTS * ROWS, 2 * HD), BF16),
            block(3), block(3), block(3), block(3), block(3), block(3),
            block(2), block(2), block(2), block(2), block(), block(),
            pltpu.VMEM((ROWS, 2 * HD), F32),
            pltpu.VMEM((ROWS, 2 * HD), F32),
            pltpu.VMEM((n_stage, SIDE * SIDE, pad_heads, HD), F32),
            pltpu.VMEM((ROWS, HD), F32),
            pltpu.VMEM((ROWS, HD), F32),
            pltpu.VMEM((ROWS, HD), jnp.int32),
            pltpu.SemaphoreType.DMA((96,)),
            pltpu.SemaphoreType.DMA((SLOTS,)),
            pltpu.SemaphoreType.DMA((SLOTS,)),
            pltpu.SemaphoreType.DMA((3, 8)),
            pltpu.SemaphoreType.DMA((n_stage, SIDE * SIDE)),
            pltpu.SemaphoreType.DMA((8,)),
        ],
        compiler_params=pltpu.CompilerParams(
            collective_id=0, has_side_effects=True, vmem_limit_bytes=56 * 1024 * 1024
        ),
        cost_estimate=pl.CostEstimate(
            flops=12 * heads * ROWS * WINDOW * ROWS * HD,
            bytes_accessed=4 * 2 * ROWS * width,
            transcendentals=heads * ROWS * WINDOW * ROWS,
        ),
    )(
        q_lin.reshape(ROWS, width), k_lin.reshape(ROWS, 2 * HD), v_lin.reshape(ROWS, 2 * HD),
        out_grad.reshape(ROWS, width), q_bias, doc_lengths, freq,
    )
    attended, grad_q, grad_k, grad_v, bias_grad = pl.pallas_call(
        write_out,
        out_shape=tuple(jax.ShapeDtypeStruct(o.shape, o.dtype) for o in outs),
        in_specs=[vmem] * 5,
        out_specs=(anywhere,) * 5,
        scratch_shapes=[pltpu.SemaphoreType.DMA((5,))],
    )(*outs)
    return (attended[None], grad_q[None], grad_k[None], grad_v[None], bias_grad)


def solution(mesh):
    rows = P("dp", "ctx", None)
    return jax.shard_map(
        shards,
        mesh=mesh,
        in_specs=(rows, rows, rows, rows, P(), P("dp", None)),
        out_specs=(rows, rows, rows, rows, P()),
        check_vma=False,
    )
```

time: 87.2 us -> 66.5 us (0.76)
  the two profiles are of different devices: /device:TPU:1 before, /device:TPU:34 now
where the time goes in v2:
time: 66.5 us; the launch traced here: 66.4 us
  Pallas kernels  65.7 us (99%)
    pallas_call x1, Pallas kernels, shards(): pl.pallas_call(lambda *refs: kernel(dp_size, group, *refs), out_shape=(ja...  63.5 us
    pallas_call x1, Pallas kernels, shards(): pl.pallas_call(write_out, out_shape=tuple((jax.ShapeDtypeStruct(o.shape,...  2.19 us

profile of v2, /device:TPU:34, one launch (start us, length us, event | category | flops | bytes accessed | tf_op | source)
XLA Modules:
  0.0 66.4 jit_solution(10105222934139694581)
XLA Ops:
  0.6 63.5 %shard_map.110 = (bf16[128,1792]{1,0:T(8,128)(2,1)}, bf16[128,1792]{1,0:T(8,128)(2,1)}, bf16[128,256]{1,0:T(8,128)(2,1)}, bf16[128,256]{1,0:T(8,128)(2,1)}, f32[1792]{0:T(1024)}) custom-call(bf16[128,1792]{1,0:T(8,128)(2,1)} %bitcast.8, bf16[128,256]{1,0:T(8,128)(2,1)} %bitcast.12, bf16[128,256]{1,0:T(8,128)(2,1)} %bitcast.13, bf16[128,1792]{1,0:T(8,128)(2,1)} %bitcast.9, ...), custom_call_target="tpu_custom_call" | custom-call | flops 3523215360 | bytes 1835008 | tf_op jit(solution)/shard_map/pallas_call | solution.py:531
  64.2 2.2 %shard_map.111 = (bf16[128,1792]{1,0:T(8,128)(2,1)}, bf16[128,1792]{1,0:T(8,128)(2,1)}, bf16[128,256]{1,0:T(8,128)(2,1)}, bf16[128,256]{1,0:T(8,128)(2,1)}, f32[1792]{0:T(1024)}) custom-call(bf16[128,1792]{1,0:T(8,128)(2,1)} %get-tuple-element.15.refs_0_, bf16[128,1792]{1,0:T(8,128)(2,1)} %get-tuple-element.16.refs_1_, ...), custom_call_target="tpu_custom_call" | custom-call | tf_op jit(solution)/shard_map/pallas_call | solution.py:585

commit v3 on v2

--- a/solution.py
+++ b/solution.py
@@ -37,9 +37,9 @@
 
 def kernel(
     dp_size, group, q_hbm, k_hbm, v_hbm, do_hbm, bias_ref, len_ref, freq_ref,
-    att_hbm, gq_hbm, gk_hbm, gv_hbm, bg_ref,
-    q_ref, k_ref, v_ref, do_ref, att_ref, gq_ref, gk_ref, gv_ref,
-    kbuf, vbuf, qs, dos, s_ref, p_ref, w_ref, ds_ref, mx_ref, acc_ref, stat_ref,
+    att_ref, gq_ref, gk_ref, gv_ref, bg_ref,
+    q_ref, k_ref, v_ref, do_ref,
+    kbuf, vbuf, qs, dos, s_ref, p_ref, w_ref, ds_ref, acc_ref,
     gkb, gvb, far_k, far_v, nl_k, nl_v, nr_k, nr_v, rz_k, rz_v, zs_k, zs_v, sp_k, sp_v,
     acck, accv, bst, cos_ref, sin_ref, start_ref,
     send_sems, krecv, vrecv, rrecv, brecv, local_sems,
@@ -99,8 +99,6 @@
     load(do_hbm, do_ref, 1)
     load(k_hbm, k_ref, 2)
     load(v_hbm, v_ref, 3)
-    pl.semaphore_wait(barrier, count)
-
     pending = []
 
     def slot(buf, s, blocks=1):
@@ -153,32 +151,32 @@
         if dr == 0:
             send(special_from, own, slot(buf, 0), recv.at[0], c + 9)
 
-    def forward(dr):
+    def forward_keys(dr):
         valid = z >= dr
         sl, sr = first(dr) + xl, first(dr) + xr
-        kl, kr, vl, vr = slot(kbuf, sl), slot(kbuf, sr), slot(vbuf, sl), slot(vbuf, sr)
+        kl, kr = slot(kbuf, sl), slot(kbuf, sr)
         use_l, use_r = need(dr, x, xl), need(dr, x, xr)
+        on = need(dr, xr, xl) & far_path(dr)
+        arrived(valid & (use_l | on), kl, krecv.at[sl])
         if far_path(dr):
-            on_v, on_k = need(dr, xl, xr), need(dr, xr, xl)
-            arrived(valid & (use_r | on_v), vr, vrecv.at[sr])
-            send(valid & on_v, vr, vr, vrecv.at[sr], left)
-            arrived(valid & (use_l | on_k), kl, krecv.at[sl])
-            send(valid & on_k, kl, kl, krecv.at[sl], right)
-        else:
-            arrived(valid & use_r, vr, vrecv.at[sr])
-            arrived(valid & use_l, kl, krecv.at[sl])
+            send(valid & on, kl, kl, krecv.at[sl], right)
+        arrived(valid & use_r, kr, krecv.at[sr])
+
+    def forward_values(dr):
+        valid = z >= dr
+        sl, sr = first(dr) + xl, first(dr) + xr
+        vl, vr = slot(vbuf, sl), slot(vbuf, sr)
+        use_l, use_r = need(dr, x, xl), need(dr, x, xr)
+        on = need(dr, xl, xr) & far_path(dr)
+        arrived(valid & (use_r | on), vr, vrecv.at[sr])
+        if far_path(dr):
+            send(valid & on, vr, vr, vrecv.at[sr], left)
         arrived(valid & use_l, vl, vrecv.at[sl])
-        arrived(valid & use_r, kr, krecv.at[sr])
-
-    def last(dr):
-        valid = z >= dr
-        so = first(dr) + xo
-        arrived(valid & need(dr, x, xo), slot(kbuf, so), krecv.at[so])
-        arrived(valid & need(dr, x, xo), slot(vbuf, so), vrecv.at[so])
-
-    loaded(v_hbm, v_ref, 3)
-    vbuf[pl.ds(pl.multiple_of((9 + x) * ROWS, ROWS), ROWS), :] = v_ref[...]
-    spread(vbuf, vrecv, False, 0)
+
+    def last(buf, recv):
+        for dr in (0, 1, 2):
+            so = first(dr) + xo
+            arrived((z >= dr) & need(dr, x, xo), slot(buf, so), recv.at[so])
 
     pos = c * ROWS + lax.broadcasted_iota(jnp.int32, (ROWS, HD), 0)
     start = jnp.zeros((ROWS, HD), jnp.int32)
@@ -205,7 +203,8 @@
     for g in range(2):
         cols = slice(g * HD, (g + 1) * HD)
         kbuf[own_rows, cols] = rope(k_ref[:, cols].astype(F32)).astype(BF16)
-    spread(kbuf, krecv, True, 0)
+    loaded(v_hbm, v_ref, 3)
+    vbuf[own_rows, :] = v_ref[...]
 
     def clear(s):
         rows = pl.ds(pl.multiple_of(s * ROWS, ROWS), ROWS)
@@ -244,8 +243,8 @@
 
     first_key = (c - (WINDOW - 1)) * ROWS
 
-    for g in range(2):
-        mx_ref[g] = jnp.full((group * ROWS, HD), FILL, F32)
+    def pair_cols(p):
+        return pl.ds(pl.multiple_of(p * 2 * ROWS, 2 * ROWS), 2 * ROWS)
 
     def score_step(p):
         key_pos = first_key + p * 2 * ROWS + lax.broadcasted_iota(jnp.int32, (ROWS, 2 * ROWS), 1)
@@ -257,112 +256,77 @@
             raw = lax.dot_general(qs[g], keys, nt, preferred_element_type=F32)
             for h in range(group):
                 rows = slice(h * ROWS, (h + 1) * ROWS)
-                part = jnp.where(visible, raw[rows], FILL)
-                s_ref[g, p, rows] = part
-                mx_ref[g, rows] = jnp.maximum(
-                    mx_ref[g, rows], jnp.maximum(part[:, :HD], part[:, HD:])
-                )
+                s_ref[g, rows, pair_cols(p)] = jnp.where(visible, raw[rows], FILL)
+        return 0
+
+    def prob_step(p):
+        for g in range(2):
             values = vbuf[window(p), g * HD : (g + 1) * HD]
-            p_ref[g, p] = lax.dot_general(dos[g], values, nt, preferred_element_type=F32)
+            p_ref[g, :, pair_cols(p)] = lax.dot_general(
+                dos[g], values, nt, preferred_element_type=F32
+            )
         return 0
 
+    pl.semaphore_wait(barrier, count)
+    spread(kbuf, krecv, True, 0)
+    spread(vbuf, vrecv, False, 0)
+    spread(kbuf, krecv, True, 1)
+    forward_keys(0)
     spread(vbuf, vrecv, False, 1)
-    spread(kbuf, krecv, True, 1)
-    forward(0)
+    forward_values(0)
+    spread(kbuf, krecv, True, 2)
+    forward_keys(1)
     spread(vbuf, vrecv, False, 2)
-    spread(kbuf, krecv, True, 2)
-    forward(1)
+    forward_values(1)
     score_step(4)
-    forward(2)
+    forward_keys(2)
     arrived(special_to, slot(kbuf, 0), krecv.at[0])
+    lax.fori_loop(0, 2, lambda i, carry: score_step(2 - 2 * i), 0)
+    prob_step(4)
+    last(kbuf, krecv)
+    lax.fori_loop(0, 2, lambda i, carry: score_step(3 - 2 * i), 0)
+
+    factor = scale * math.log2(math.e)
+
+    whole = pl.ds(pl.multiple_of(x * ROWS, ROWS), WINDOW * ROWS)
+    chunk = ROWS // 4
+
+    def softmax_step(h, carry):
+        for g in range(2):
+            for r in range(4):
+                rows = pl.ds(pl.multiple_of(h * ROWS, ROWS) + r * chunk, chunk)
+                scores = s_ref[g, rows, :]
+                top = jnp.max(scores, axis=1, keepdims=True)
+                terms = jnp.exp2((scores - top) * factor)
+                total = jnp.sum(terms, axis=1, keepdims=True)
+                w_ref[g, rows, :] = (terms * (1.0 / total)).astype(BF16)
+        return carry
+
+    lax.fori_loop(0, group, softmax_step, 0)
+    forward_values(2)
     arrived(special_to, slot(vbuf, 0), vrecv.at[0])
-    lax.fori_loop(0, 2, lambda i, carry: score_step(2 - 2 * i), 0)
-    last(0)
-    last(1)
-    last(2)
-    lax.fori_loop(0, 2, lambda i, carry: score_step(3 - 2 * i), 0)
-
-    factor = scale * math.log2(math.e)
-
+    last(vbuf, vrecv)
+    lax.fori_loop(0, PAIRS - 1, lambda p, carry: prob_step(p), 0)
     for g in range(2):
-        for h in range(group):
-            rows = slice(h * ROWS, (h + 1) * ROWS)
-            top = jnp.max(mx_ref[g, rows], axis=1, keepdims=True)
-            mx_ref[g, rows] = jnp.broadcast_to(top, (ROWS, HD))
-        acc_ref[g] = jnp.zeros((group * ROWS, HD), F32)
-
-    def exp_step(p, carry):
+        values = vbuf[whole, g * HD : (g + 1) * HD]
+        acc_ref[g] = lax.dot_general(w_ref[g], values, nn, preferred_element_type=F32)
+
+    _, at_0, _ = peer(*stages[0], 1)
+
+    def dscore_step(h, carry):
         for g in range(2):
-            for h in range(group):
-                rows = slice(h * ROWS, (h + 1) * ROWS)
-                top = mx_ref[g, rows]
-                lo = jnp.exp2((s_ref[g, p, rows, :HD] - top) * factor)
-                hi = jnp.exp2((s_ref[g, p, rows, HD:] - top) * factor)
-                s_ref[g, p, rows, :HD] = lo
-                s_ref[g, p, rows, HD:] = hi
-                acc_ref[g, rows] += lo + hi
+            cols = pl.ds(pl.multiple_of((g * group + h) * HD, HD), HD)
+            for r in range(4):
+                rows = pl.ds(pl.multiple_of(h * ROWS, ROWS) + r * chunk, chunk)
+                attended = acc_ref[g, rows, :].astype(BF16)
+                att_ref[r * chunk : (r + 1) * chunk, cols] = attended
+                product = dos[g, rows, :].astype(F32) * attended.astype(F32)
+                delta = jnp.sum(product, axis=1, keepdims=True)
+                weights = w_ref[g, rows, :].astype(F32)
+                ds_ref[g, rows, :] = (weights * (p_ref[g, rows, :] - delta)).astype(BF16)
         return carry
 
-    lax.fori_loop(0, PAIRS, exp_step, 0)
-
-    for g in range(2):
-        for h in range(group):
-            rows = slice(h * ROWS, (h + 1) * ROWS)
-            total = jnp.sum(acc_ref[g, rows], axis=1, keepdims=True)
-            stat_ref[g, rows] = jnp.broadcast_to(1.0 / total, (ROWS, HD))
-        acc_ref[g] = jnp.zeros((group * ROWS, HD), F32)
-
-    def out_step(p, carry):
-        for g in range(2):
-            inverse = stat_ref[g]
-            lo = (s_ref[g, p, :, :HD] * inverse).astype(BF16)
-            hi = (s_ref[g, p, :, HD:] * inverse).astype(BF16)
-            weights = jnp.concatenate([lo, hi], axis=1)
-            w_ref[g, p] = weights
-            values = vbuf[window(p), g * HD : (g + 1) * HD]
-            acc_ref[g] += lax.dot_general(weights, values, nn, preferred_element_type=F32)
-        return carry
-
-    lax.fori_loop(0, PAIRS, out_step, 0)
-
-    for g in range(2):
-        for h in range(group):
-            rows = slice(h * ROWS, (h + 1) * ROWS)
-            attended = acc_ref[g, rows].astype(BF16)
-            at = (g * group + h) * HD
-            att_ref[:, at : at + HD] = attended
-            delta = jnp.sum(
-                dos[g, rows].astype(F32) * attended.astype(F32), axis=1, keepdims=True
-            )
-            stat_ref[g, rows] = jnp.broadcast_to(delta, (ROWS, HD))
-        acc_ref[g] = jnp.zeros((group * ROWS, HD), F32)
-
-    load(att_ref, att_hbm, 4)
-    _, at_0, _ = peer(*stages[0], 1)
-
-    def dscore_step(p, carry):
-        for g in range(2):
-            keys = kbuf[window(p), g * HD : (g + 1) * HD]
-            delta = stat_ref[g]
-            lo = w_ref[g, p, :, :HD].astype(F32) * (p_ref[g, p, :, :HD] - delta)
-            hi = w_ref[g, p, :, HD:].astype(F32) * (p_ref[g, p, :, HD:] - delta)
-            dscore = jnp.concatenate([lo.astype(BF16), hi.astype(BF16)], axis=1)
-            ds_ref[g, p] = dscore
-            acc_ref[g] += lax.dot_general(dscore, keys, nn, preferred_element_type=F32)
-        return carry
-
-    lax.fori_loop(0, PAIRS, dscore_step, 0)
-    for h in range(heads):
-        g, r = h // group, (h % group) * ROWS
-        cols = slice(h * HD, (h + 1) * HD)
-        before = rope_back(scale * acc_ref[g, r : r + ROWS])
-        gq_ref[:, cols] = before.astype(BF16)
-        bst[0, at_0, h : h + 1, :] = jnp.sum(before, axis=0, keepdims=True)
-    pad = bst.shape[2] - heads
-    if pad:
-        bst[0, at_0, heads:, :] = jnp.zeros((pad, HD), F32)
-    load(gq_ref, gq_hbm, 5)
-
+    lax.fori_loop(0, group, dscore_step, 0)
     def bias_start(i):
         kind, size = stages[i]
         for step in range(1, size):
@@ -386,13 +350,15 @@
             for h in range(heads):
                 bg_ref[h * HD : (h + 1) * HD] = total[h]
 
-    bias_start(0)
-
     def term_step(p, carry):
         for g in range(2):
             cols = slice(g * HD, (g + 1) * HD)
-            key_term = lax.dot_general(ds_ref[g, p], qs[g], tn, preferred_element_type=F32)
-            value_term = lax.dot_general(w_ref[g, p], dos[g], tn, preferred_element_type=F32)
+            key_term = lax.dot_general(
+                ds_ref[g, :, pair_cols(p)], qs[g], tn, preferred_element_type=F32
+            )
+            value_term = lax.dot_general(
+                w_ref[g, :, pair_cols(p)], dos[g], tn, preferred_element_type=F32
+            )
             gkb[window(p), cols] = (scale * key_term).astype(BF16)
             gvb[window(p), cols] = value_term.astype(BF16)
         return carry
@@ -466,6 +432,21 @@
     begin_pair = jnp.where(x < 2, 2, 1)
     lax.fori_loop(0, 3, lambda i, carry: term_step(begin_pair + i, carry), 0)
     back_far(1)
+
+    for g in range(2):
+        keys = kbuf[whole, g * HD : (g + 1) * HD]
+        acc_ref[g] = lax.dot_general(ds_ref[g], keys, nn, preferred_element_type=F32)
+    for h in range(heads):
+        g, r = h // group, (h % group) * ROWS
+        cols = slice(h * HD, (h + 1) * HD)
+        before = rope_back(scale * acc_ref[g, r : r + ROWS])
+        gq_ref[:, cols] = before.astype(BF16)
+        bst[0, at_0, h : h + 1, :] = jnp.sum(before, axis=0, keepdims=True)
+    pad = bst.shape[2] - heads
+    if pad:
+        bst[0, at_0, heads:, :] = jnp.zeros((pad, HD), F32)
+    bias_start(0)
+
     end_pair = jnp.where(x < 2, 1, PAIRS - 1)
     lax.fori_loop(0, 2, lambda i, carry: term_step(i * end_pair, carry), 0)
     back_far(0)
@@ -490,13 +471,7 @@
         cols = slice(g * HD, (g + 1) * HD)
         gk_ref[:, cols] = rope_back(acck[:, cols]).astype(BF16)
     gv_ref[...] = accv[...].astype(BF16)
-    load(gk_ref, gk_hbm, 6)
-    load(gv_ref, gv_hbm, 7)
     bias_end(len(stages) - 1)
-    loaded(att_ref, att_hbm, 4)
-    loaded(gq_ref, gq_hbm, 5)
-    loaded(gk_ref, gk_hbm, 6)
-    loaded(gv_ref, gv_hbm, 7)
 
     for pred, copy in pending:
 
@@ -506,7 +481,7 @@
 
 
 def write_out(*refs):
-    sems = refs[-1]
+    sems = refs[10]
     copies = [pltpu.make_async_copy(refs[i], refs[5 + i], sems.at[i]) for i in range(5)]
     for copy in copies:
         copy.start()
@@ -531,27 +506,24 @@
     outs = pl.pallas_call(
         lambda *refs: kernel(dp_size, group, *refs),
         out_shape=(
-            jax.ShapeDtypeStruct((ROWS, width), BF16),
-            jax.ShapeDtypeStruct((ROWS, width), BF16),
-            jax.ShapeDtypeStruct((ROWS, 2 * HD), BF16),
-            jax.ShapeDtypeStruct((ROWS, 2 * HD), BF16),
-            jax.ShapeDtypeStruct((width,), F32),
+            pltpu.VMEM((ROWS, width), BF16),
+            pltpu.VMEM((ROWS, width), BF16),
+            pltpu.VMEM((ROWS, 2 * HD), BF16),
+            pltpu.VMEM((ROWS, 2 * HD), BF16),
+            pltpu.VMEM((width,), F32),
         ),
         in_specs=[anywhere] * 4 + [vmem, pl.BlockSpec(memory_space=pltpu.SMEM), vmem],
-        out_specs=(anywhere,) * 4 + (vmem,),
+        out_specs=(vmem,) * 5,
         scratch_shapes=[
             pltpu.VMEM((ROWS, width), BF16), block(), block(), pltpu.VMEM((ROWS, width), BF16),
-            pltpu.VMEM((ROWS, width), BF16), pltpu.VMEM((ROWS, width), BF16), block(), block(),
             pltpu.VMEM((SLOTS * ROWS, 2 * HD), BF16),
             pltpu.VMEM((SLOTS * ROWS, 2 * HD), BF16),
             pltpu.VMEM((2, rows, HD), BF16),
             pltpu.VMEM((2, rows, HD), BF16),
-            pltpu.VMEM((2, PAIRS, rows, 2 * ROWS), F32),
-            pltpu.VMEM((2, PAIRS, rows, 2 * ROWS), F32),
-            pltpu.VMEM((2, PAIRS, rows, 2 * ROWS), BF16),
-            pltpu.VMEM((2, PAIRS, rows, 2 * ROWS), BF16),
-            pltpu.VMEM((2, rows, HD), F32),
-            pltpu.VMEM((2, rows, HD), F32),
+            pltpu.VMEM((2, rows, WINDOW * ROWS), F32),
+            pltpu.VMEM((2, rows, WINDOW * ROWS), F32),
+            pltpu.VMEM((2, rows, WINDOW * ROWS), BF16),
+            pltpu.VMEM((2, rows, WINDOW * ROWS), BF16),
             pltpu.VMEM((2, rows, HD), F32),
             pltpu.VMEM((SLOTS * ROWS, 2 * HD), BF16),
             pltpu.VMEM((SLOTS * ROWS, 2 * HD), BF16),
@@ -588,7 +560,7 @@
         in_specs=[vmem] * 5,
         out_specs=(anywhere,) * 5,
         scratch_shapes=[pltpu.SemaphoreType.DMA((5,))],
-    )(*outs)
+    )(*(pltpu.with_memory_space_constraint(o, pltpu.VMEM) for o in outs))
     return (attended[None], grad_q[None], grad_k[None], grad_v[None], bias_grad)
 
 

time: 66.5 us -> 63.9 us (0.961)
  the two profiles are of different devices: /device:TPU:34 before, /device:TPU:1 now
where the time goes in v3:
time: 63.9 us; the launch traced here: 63.6 us
  Pallas kernels  63 us (99%)
  between operations  0.64 us (1%)
    pallas_call x1, Pallas kernels, shards(): pl.pallas_call(lambda *refs: kernel(dp_size, group, *refs), out_shape=(pl...  62 us

profile of v3, /device:TPU:1, one launch (start us, length us, event | category | flops | bytes accessed | tf_op | source)
XLA Modules:
  0.0 63.6 jit_solution(13968177911780954992)
XLA Ops:
  0.6 62.0 %shard_map.110 = (bf16[128,1792]{1,0:T(8,128)(2,1)S(1)}, bf16[128,1792]{1,0:T(8,128)(2,1)S(1)}, bf16[128,256]{1,0:T(8,128)(2,1)S(1)}, bf16[128,256]{1,0:T(8,128)(2,1)S(1)}, f32[1792]{0:T(1024)S(1)}) custom-call(bf16[128,1792]{1,0:T(8,128)(2,1)} %bitcast.8, bf16[128,256]{1,0:T(8,128)(2,1)} %bitcast.12, bf16[128,256]{1,0:T(8,128)(2,1)} %bitcast.13, ...), custom_call_target="tpu_custom_call" | custom-call | flops 3523215360 | bytes 1835008 | tf_op jit(solution)/shard_map/pallas_call | solution.py:506
  62.6 1.0 %shard_map.111 = (bf16[128,1792]{1,0:T(8,128)(2,1)}, bf16[128,1792]{1,0:T(8,128)(2,1)}, bf16[128,256]{1,0:T(8,128)(2,1)}, bf16[128,256]{1,0:T(8,128)(2,1)}, f32[1792]{0:T(1024)}) custom-call(bf16[128,1792]{1,0:T(8,128)(2,1)S(1)} %get-tuple-element.15.refs_0_, bf16[128,1792]{1,0:T(8,128)(2,1)S(1)} %get-tuple-element.16.refs_1_, ...), custom_call_target="tpu_custom_call" | custom-call | tf_op jit(solution)/shard_map/pallas_call | solution.py:557

commit v4 on v3

--- a/solution.py
+++ b/solution.py
@@ -11,6 +11,7 @@
 HD = 128
 ROWS = 128
 SIDE = 4
+NEAR = 4
 WINDOW = 10
 SLOTS = 13
 PAIRS = WINDOW // 2
@@ -42,7 +43,7 @@
     kbuf, vbuf, qs, dos, s_ref, p_ref, w_ref, ds_ref, acc_ref,
     gkb, gvb, far_k, far_v, nl_k, nl_v, nr_k, nr_v, rz_k, rz_v, zs_k, zs_v, sp_k, sp_v,
     acck, accv, bst, cos_ref, sin_ref, start_ref,
-    send_sems, krecv, vrecv, rrecv, brecv, local_sems,
+    send_sems, krecv, vrecv, rrecv, brecv, local_sems, relay_sem,
 ):
     c = lax.axis_index("ctx")
     d = lax.axis_index("dp")
@@ -82,10 +83,11 @@
 
     count = jnp.where(special_from | special_to, 1, 0)
     for kind, size in stages:
-        for step in range(1, size):
+        greeted = [s for s in range(1, size) if min(s, size - s) <= NEAR or kind != "z"]
+        for step in greeted:
             target, _, _ = peer(kind, size, step)
             pl.semaphore_signal(barrier, inc=1, device_id=target, device_id_type=MESH)
-        count = count + (size - 1)
+        count = count + len(greeted)
 
     @pl.when(special_from)
     def _():
@@ -268,6 +270,12 @@
         return 0
 
     pl.semaphore_wait(barrier, count)
+    kind, size = stages[0]
+    relayed = size > 2 * NEAR
+    if relayed:
+        for step in (NEAR, size - NEAR):
+            target, _, _ = peer(kind, size, step)
+            pl.semaphore_signal(relay_sem, inc=1, device_id=target, device_id_type=MESH)
     spread(kbuf, krecv, True, 0)
     spread(vbuf, vrecv, False, 0)
     spread(kbuf, krecv, True, 1)
@@ -369,6 +377,10 @@
         to_k, to_v = (left, right) if far_path(dr) else (base + xo, base + xo)
         send(pred, slot(gkb, so), far_k.at[dr], rrecv.at[dr, 0], to_k)
         send(pred, slot(gvb, so), far_v.at[dr], rrecv.at[dr, 1], to_v)
+        valid = z >= dr
+        to_l, to_r = valid & need(dr, x, xl), valid & need(dr, x, xr)
+        send(to_l, slot(gvb, first(dr) + xl), nr_v.at[dr], rrecv.at[dr, 3], left)
+        send(to_r, slot(gkb, first(dr) + xr), nl_k.at[dr], rrecv.at[dr, 4], right)
 
     def add_into(buf, s, other):
         rows = pl.ds(pl.multiple_of(s * ROWS, ROWS), ROWS)
@@ -378,8 +390,6 @@
         valid = z >= dr
         sl, sr = first(dr) + xl, first(dr) + xr
         to_l, to_r = valid & need(dr, x, xl), valid & need(dr, x, xr)
-        send(to_l, slot(gvb, sl), nr_v.at[dr], rrecv.at[dr, 3], left)
-        send(to_r, slot(gkb, sr), nl_k.at[dr], rrecv.at[dr, 4], right)
         if not far_path(dr):
             send(to_l, slot(gkb, sl), nr_k.at[dr], rrecv.at[dr, 2], left)
             send(to_r, slot(gvb, sr), nl_v.at[dr], rrecv.at[dr, 5], right)
@@ -445,6 +455,8 @@
     pad = bst.shape[2] - heads
     if pad:
         bst[0, at_0, heads:, :] = jnp.zeros((pad, HD), F32)
+    if relayed:
+        pl.semaphore_wait(relay_sem, 2)
     bias_start(0)
 
     end_pair = jnp.where(x < 2, 1, PAIRS - 1)
@@ -458,9 +470,9 @@
     bias_end(0)
     back_near(0)
     back_sum(2)
+    back_sum(1)
     if len(stages) > 2:
         bias_end(1)
-    back_sum(1)
     back_sum(0)
     for dr in (2, 1):
         add_when(z + dr < SIDE, acck, rz_k.at[dr - 1], rrecv.at[dr, 6])
@@ -541,6 +553,7 @@
             pltpu.SemaphoreType.DMA((3, 8)),
             pltpu.SemaphoreType.DMA((n_stage, SIDE * SIDE)),
             pltpu.SemaphoreType.DMA((8,)),
+            pltpu.SemaphoreType.REGULAR,
         ],
         compiler_params=pltpu.CompilerParams(
             collective_id=0, has_side_effects=True, vmem_limit_bytes=56 * 1024 * 1024

time: 63.9 us -> 62.3 us (0.975)
  Pallas kernels: 63 us -> 61.5 us
    pallas_call x1, Pallas kernels: 62 us -> 60.5 us  [shards(): pl.pallas_call(lambda *refs: kernel(dp_size, group, *refs), out_shape=(pl...]
where the time goes in v4:
time: 62.3 us; the launch traced here: 62.1 us
  Pallas kernels  61.5 us (99%)
  between operations  0.64 us (1%)
    pallas_call x1, Pallas kernels, shards(): pl.pallas_call(lambda *refs: kernel(dp_size, group, *refs), out_shape=(pl...  60.5 us

profile of v4, /device:TPU:1, one launch (start us, length us, event | category | flops | bytes accessed | tf_op | source)
XLA Modules:
  0.0 62.1 jit_solution(13625103558127360452)
XLA Ops:
  0.6 60.5 %shard_map.110 = (bf16[128,1792]{1,0:T(8,128)(2,1)S(1)}, bf16[128,1792]{1,0:T(8,128)(2,1)S(1)}, bf16[128,256]{1,0:T(8,128)(2,1)S(1)}, bf16[128,256]{1,0:T(8,128)(2,1)S(1)}, f32[1792]{0:T(1024)S(1)}) custom-call(bf16[128,1792]{1,0:T(8,128)(2,1)} %bitcast.8, bf16[128,256]{1,0:T(8,128)(2,1)} %bitcast.12, bf16[128,256]{1,0:T(8,128)(2,1)} %bitcast.13, ...), custom_call_target="tpu_custom_call" | custom-call | flops 3523215360 | bytes 1835008 | tf_op jit(solution)/shard_map/pallas_call | solution.py:518
  61.1 1.0 %shard_map.111 = (bf16[128,1792]{1,0:T(8,128)(2,1)}, bf16[128,1792]{1,0:T(8,128)(2,1)}, bf16[128,256]{1,0:T(8,128)(2,1)}, bf16[128,256]{1,0:T(8,128)(2,1)}, f32[1792]{0:T(1024)}) custom-call(bf16[128,1792]{1,0:T(8,128)(2,1)S(1)} %get-tuple-element.15.refs_0_, bf16[128,1792]{1,0:T(8,128)(2,1)S(1)} %get-tuple-element.16.refs_1_, ...), custom_call_target="tpu_custom_call" | custom-call | tf_op jit(solution)/shard_map/pallas_call | solution.py:570

commit v5 on v4

--- a/solution.py
+++ b/solution.py
@@ -439,9 +439,9 @@
             send(valid, zs_k.at[dr - 1], rz_k.at[dr - 1], rrecv.at[dr, 6], down)
             send(valid, zs_v.at[dr - 1], rz_v.at[dr - 1], rrecv.at[dr, 7], down)
 
-    begin_pair = jnp.where(x < 2, 2, 1)
-    lax.fori_loop(0, 3, lambda i, carry: term_step(begin_pair + i, carry), 0)
-    back_far(1)
+    lax.fori_loop(0, 3, term_step, 0)
+    back_far(2)
+    back_near(2)
 
     for g in range(2):
         keys = kbuf[whole, g * HD : (g + 1) * HD]
@@ -459,11 +459,9 @@
         pl.semaphore_wait(relay_sem, 2)
     bias_start(0)
 
-    end_pair = jnp.where(x < 2, 1, PAIRS - 1)
-    lax.fori_loop(0, 2, lambda i, carry: term_step(i * end_pair, carry), 0)
+    lax.fori_loop(3, PAIRS, term_step, 0)
+    back_far(1)
     back_far(0)
-    back_far(2)
-    back_near(2)
     send(special_to, slot(gkb, 0), sp_k, rrecv.at[0, 6], c - 9)
     send(special_to, slot(gvb, 0), sp_v, rrecv.at[0, 7], c - 9)
     back_near(1)

time: 62.3 us -> 62.2 us (level)
  no operation moved by 1% of the time
where the time goes in v5:
time: 62.2 us; the launch traced here: 62 us
  Pallas kernels  61.4 us (99%)
  between operations  0.64 us (1%)
    pallas_call x1, Pallas kernels, shards(): pl.pallas_call(lambda *refs: kernel(dp_size, group, *refs), out_shape=(pl...  60.4 us

profile of v5, /device:TPU:1, one launch (start us, length us, event | category | flops | bytes accessed | tf_op | source)
XLA Modules:
  0.0 62.0 jit_solution(2562466544872967099)
XLA Ops:
  0.6 60.4 %shard_map.110 = (bf16[128,1792]{1,0:T(8,128)(2,1)S(1)}, bf16[128,1792]{1,0:T(8,128)(2,1)S(1)}, bf16[128,256]{1,0:T(8,128)(2,1)S(1)}, bf16[128,256]{1,0:T(8,128)(2,1)S(1)}, f32[1792]{0:T(1024)S(1)}) custom-call(bf16[128,1792]{1,0:T(8,128)(2,1)} %bitcast.8, bf16[128,256]{1,0:T(8,128)(2,1)} %bitcast.12, bf16[128,256]{1,0:T(8,128)(2,1)} %bitcast.13, ...), custom_call_target="tpu_custom_call" | custom-call | flops 3523215360 | bytes 1835008 | tf_op jit(solution)/shard_map/pallas_call | solution.py:516
  61.0 1.0 %shard_map.111 = (bf16[128,1792]{1,0:T(8,128)(2,1)}, bf16[128,1792]{1,0:T(8,128)(2,1)}, bf16[128,256]{1,0:T(8,128)(2,1)}, bf16[128,256]{1,0:T(8,128)(2,1)}, f32[1792]{0:T(1024)}) custom-call(bf16[128,1792]{1,0:T(8,128)(2,1)S(1)} %get-tuple-element.15.refs_0_, bf16[128,1792]{1,0:T(8,128)(2,1)S(1)} %get-tuple-element.16.refs_1_, ...), custom_call_target="tpu_custom_call" | custom-call | tf_op jit(solution)/shard_map/pallas_call | solution.py:568
